TPU v7x, 32 devices: a whole 2x2x4 slice. The times are simulated.
32 devices in a mesh: dp: 8 (over z, y), tensor: 4 (over x, core).
Axes of the slice: x: 2, y: 2, z: 4, core: 2. Of those that a mesh axis runs over, the one named last changes fastest.
Arguments:
- inputs: bfloat16 [32, 197, 768], P(('dp', 'tensor')), may hold values from -6 to 6
- ln1_gain: bfloat16 [768], P('dp'), may hold values from 0.5 to 1.5
- ln1_bias: bfloat16 [768], P('dp'), may hold values from -3 to 3
- qkv_weight: bfloat16 [768, 3, 768], P('dp', None, 'tensor'), may hold values from -0.21875 to 0.21875
- proj_weight: bfloat16 [768, 768], P('tensor', 'dp'), may hold values from -1.5 to 1.5
- proj_bias: bfloat16 [768], P('dp'), may hold values from -1.5 to 1.5
- ln2_gain: bfloat16 [768], P('dp'), may hold values from 0.5 to 1.5
- ln2_bias: bfloat16 [768], P('dp'), may hold values from -3 to 3
- router_weight: bfloat16 [768, 4], P('dp'), may hold values from -0.15625 to 0.15625
- expert_in: bfloat16 [4, 768, 3072], P(None, 'dp', 'tensor'), may hold values from -0.21875 to 0.21875
- expert_in_bias: bfloat16 [4, 3072], P(None, 'tensor'), may hold values from -1.5 to 1.5
- expert_out: bfloat16 [4, 3072, 768], P(None, 'tensor', 'dp'), may hold values from -0.4375 to 0.4375
- expert_out_bias: bfloat16 [4, 768], P(None, 'dp'), may hold values from -4 to 4
- expert_ids: int32 [32, 197, 2], P('dp'), may hold values from 0 to 3, as said below
- slot_ids: int32 [32, 197, 2], P('dp'), may hold values from 0 to 414, as said below
- cotangent: bfloat16 [32, 197, 768], P(('dp', 'tensor')), may hold values from -6 to 6
Outputs:
- block_out: bfloat16 [32, 197, 768], P(('dp', 'tensor'))
- input_grad: float32 [32, 197, 768], P(('dp', 'tensor'))
- ln1_gain_grad: float32 [768], P('dp')
- ln1_bias_grad: float32 [768], P('dp')
- qkv_weight_grad: float32 [768, 3, 768], P('dp', None, 'tensor')
- proj_weight_grad: float32 [768, 768], P('tensor', 'dp')
- proj_bias_grad: float32 [768], P('dp')
- ln2_gain_grad: float32 [768], P('dp')
- ln2_bias_grad: float32 [768], P('dp')
- router_grad: float32 [768, 4], P('dp')
- expert_in_grad: float32 [4, 768, 3072], P(None, 'dp', 'tensor')
- expert_in_bias_grad: float32 [4, 3072], P(None, ('dp', 'tensor'))
- expert_out_grad: float32 [4, 3072, 768], P(None, 'tensor', 'dp')
- expert_out_bias_grad: float32 [4, 768], P(None, 'dp')
Inputs may be any that keep to these rules, and one draw needn't show every extreme that they name: `expert_ids`: the two experts of a token differ. Within one group of 4 images (one index of dp) every pair of expert and slot is used at most once, an expert's used slots are 0 up to its count less one, and one expert uses all 415 slots. `slot_ids`: the slot that goes with expert_ids of the same entry.
All inputs are finite; a program needn't handle non-finite values.
Results may differ from a plain program's by a relative error of at most 0.013.
Values may be sent and summed in bfloat16 or wider, within the bound.
A program may use at most 128 MiB of HBM per device.

v0:
```python
import jax
import jax.numpy as jnp
from jax import lax
from jax.sharding import PartitionSpec as P

HEAD_DIM = 64
SEQ = 197


EPSILON = 1e-06
PRECISE = lax.Precision.HIGHEST


def layer_norm(values, gain, bias):
    centred = values - jnp.mean(values, axis=-1, keepdims=True)
    spread = jnp.mean(centred * centred, axis=-1, keepdims=True)
    return centred * lax.rsqrt(spread + EPSILON) * gain + bias


def gelu_tanh(values):
    return jax.nn.gelu(values, approximate=True)


def per_device(
    inputs,
    ln1_gain,
    ln1_bias,
    qkv_weight,
    proj_weight,
    proj_bias,
    ln2_gain,
    ln2_bias,
    router_weight,
    expert_in,
    expert_in_bias,
    expert_out,
    expert_out_bias,
    expert_ids,
    slot_ids,
    cotangent,
):
    local_images, seq_len, model_width = inputs.shape
    tensor_count = lax.axis_size("tensor")
    dp_count = lax.axis_size("dp")
    tensor_rank = lax.axis_index("tensor")
    dp_rank = lax.axis_index("dp")
    group_images = local_images * tensor_count
    experts = expert_in.shape[0]
    tokens = group_images * SEQ
    slot_count = 40 * tokens // (19 * experts) + 1
    heads_local = qkv_weight.shape[2] // HEAD_DIM
    score_scale = HEAD_DIM ** (-0.5)

    def own_rows(values):
        return lax.dynamic_slice_in_dim(values, tensor_rank * local_images, local_images, 0)

    def fetch_attention():
        return (
            lax.all_gather(qkv_weight, "dp", axis=0, tiled=True),
            lax.all_gather(proj_weight, "dp", axis=1, tiled=True),
            lax.all_gather(ln1_gain, "dp", axis=0, tiled=True),
            lax.all_gather(ln1_bias, "dp", axis=0, tiled=True),
            lax.all_gather(proj_bias, "dp", axis=0, tiled=True),
        )

    def fetch_experts():
        return (
            lax.all_gather(expert_in, "dp", axis=1, tiled=True),
            lax.all_gather(expert_out, "dp", axis=2, tiled=True),
            lax.all_gather(router_weight, "dp", axis=0, tiled=True),
            lax.all_gather(expert_out_bias, "dp", axis=1, tiled=True),
            lax.all_gather(ln2_gain, "dp", axis=0, tiled=True),
            lax.all_gather(ln2_bias, "dp", axis=0, tiled=True),
        )

    def scores_of(query_heads, key_heads):
        return (
            jnp.einsum(
                "bqhe,bkhe->bhqk", query_heads, key_heads, preferred_element_type=jnp.float32
            )
            * score_scale
        )

    qkv_full, proj_full, gain_one, bias_one, proj_shift = fetch_attention()
    gain_one_f = gain_one.astype(jnp.float32)
    bias_one_f = bias_one.astype(jnp.float32)
    source = inputs.astype(jnp.float32)
    normed_one = layer_norm(source, gain_one_f, bias_one_f).astype(jnp.bfloat16)
    rows_one = lax.all_gather(normed_one, "tensor", axis=0, tiled=True)
    mixed = jnp.einsum(
        "bsd,dkf->bskf", rows_one, qkv_full, preferred_element_type=jnp.float32
    ).astype(jnp.bfloat16)
    head_blocks = mixed.reshape(group_images, seq_len, 3, heads_local, HEAD_DIM)
    query_heads = head_blocks[:, :, 0]
    key_heads = head_blocks[:, :, 1]
    value_heads = head_blocks[:, :, 2]
    scores = scores_of(query_heads, key_heads)
    top_score = jnp.max(scores, axis=-1, keepdims=True)
    raised = jnp.exp(scores - top_score)
    row_total = jnp.sum(raised, axis=-1, keepdims=True)
    weights = raised / row_total
    log_total = top_score + jnp.log(row_total)
    attended = jnp.einsum(
        "bhqk,bkhe->bqhe",
        weights.astype(jnp.bfloat16),
        value_heads,
        preferred_element_type=jnp.float32,
    )
    attended = attended.astype(jnp.bfloat16).reshape(group_images, seq_len, heads_local * HEAD_DIM)
    attn_terms = jnp.einsum("bsf,fd->bsd", attended, proj_full, preferred_element_type=jnp.float32)
    attn_sum = lax.psum_scatter(attn_terms, "tensor", scatter_dimension=0, tiled=True)
    state = source + attn_sum + proj_shift.astype(jnp.float32)
    in_full, out_full, router_full, back_shift, gain_two, bias_two = fetch_experts()
    gain_two_f = gain_two.astype(jnp.float32)
    bias_two_f = bias_two.astype(jnp.float32)
    normed_two = layer_norm(state, gain_two_f, bias_two_f).astype(jnp.bfloat16)
    rows_two = lax.all_gather(normed_two, "tensor", axis=0, tiled=True)
    token_rows = rows_two.reshape(tokens, model_width)
    choice_ids = expert_ids.reshape(tokens, 2)
    places_flat = (choice_ids * slot_count + slot_ids.reshape(tokens, 2)).reshape(2 * tokens)
    logits = jnp.dot(token_rows, router_full, preferred_element_type=jnp.float32)
    router_probs = jax.nn.softmax(logits, axis=-1)
    choice_onehot = (choice_ids[:, :, None] == jnp.arange(experts)[None, None, :]).astype(
        jnp.float32
    )
    gate_values = jnp.sum(router_probs[:, None, :] * choice_onehot, axis=-1)
    owners = (
        jnp.full((experts * slot_count,), 2 * tokens, jnp.int32)
        .at[places_flat]
        .set(jnp.arange(2 * tokens, dtype=jnp.int32))
    )
    token_rows_ext = jnp.concatenate(
        [token_rows, jnp.zeros((1, model_width), jnp.bfloat16)], axis=0
    )
    dispatched = token_rows_ext[owners // 2].reshape(experts, slot_count, model_width)
    pre = (
        jnp.einsum("ecd,edf->ecf", dispatched, in_full, preferred_element_type=jnp.float32)
        + expert_in_bias.astype(jnp.float32)[:, None, :]
    )
    hidden = gelu_tanh(pre).astype(jnp.bfloat16)
    expert_terms = jnp.einsum(
        "ecf,efd->ecd", hidden, out_full, preferred_element_type=jnp.float32
    ).reshape(experts * slot_count, model_width)
    picked = expert_terms[places_flat].reshape(tokens, 2, model_width)
    mixed_terms = jnp.sum(gate_values[:, :, None] * picked, axis=1)
    mixed_sum = lax.psum_scatter(
        mixed_terms.reshape(group_images, seq_len, model_width),
        "tensor",
        scatter_dimension=0,
        tiled=True,
    )
    gates_own = own_rows(gate_values.reshape(group_images, seq_len, 2))
    onehot_own = own_rows(choice_onehot.reshape(group_images, seq_len, 2, experts))
    back_own = jnp.einsum(
        "bpke,ed->bpkd", onehot_own, back_shift.astype(jnp.float32), precision=PRECISE
    )
    shift_own = jnp.sum(gates_own[..., None] * back_own, axis=2)
    result = state + mixed_sum + shift_own
    block_out = result.astype(jnp.bfloat16)
    out_rows = lax.all_gather(cotangent, "tensor", axis=0, tiled=True)
    grad_rows = out_rows.reshape(tokens, model_width).astype(jnp.float32)
    own_grad = cotangent.astype(jnp.float32)
    refetched = fetch_experts()
    in_back, out_back, router_back = (refetched[0], refetched[1], refetched[2])
    weighted = (
        (gate_values[:, :, None] * grad_rows[:, None, :])
        .astype(jnp.bfloat16)
        .reshape(2 * tokens, model_width)
    )
    weighted = jnp.concatenate([weighted, jnp.zeros((1, model_width), jnp.bfloat16)], axis=0)
    slot_grad = weighted[owners].reshape(experts, slot_count, model_width)
    out_grad = jnp.einsum("ecf,ecd->efd", hidden, slot_grad, preferred_element_type=jnp.float32)
    hidden_grad = jnp.einsum(
        "ecd,efd->ecf", slot_grad, out_back, preferred_element_type=jnp.float32
    )
    gelu_pull = jax.vjp(gelu_tanh, pre)[1]
    pre_grad = gelu_pull(hidden_grad)[0].astype(jnp.bfloat16)
    in_grad = jnp.einsum("ecd,ecf->edf", dispatched, pre_grad, preferred_element_type=jnp.float32)
    in_bias_grad = jnp.sum(pre_grad.astype(jnp.float32), axis=1)
    in_part, out_part = (
        lax.psum_scatter(in_grad, "dp", scatter_dimension=1, tiled=True),
        lax.psum_scatter(out_grad, "dp", scatter_dimension=2, tiled=True),
    )
    slot_back = jnp.einsum(
        "ecf,edf->ecd", pre_grad, in_back, preferred_element_type=jnp.float32
    ).reshape(experts * slot_count, model_width)
    row_back = jnp.sum(slot_back[places_flat].reshape(tokens, 2, model_width), axis=1)
    gate_part = jnp.sum(grad_rows[:, None, :] * picked, axis=-1)
    row_sum, gate_sum = (
        lax.psum_scatter(
            row_back.reshape(group_images, seq_len, model_width),
            "tensor",
            scatter_dimension=0,
            tiled=True,
        ),
        lax.psum_scatter(
            gate_part.reshape(group_images, seq_len, 2), "tensor", scatter_dimension=0, tiled=True
        ),
    )
    gate_grad = gate_sum + jnp.sum(own_grad[:, :, None, :] * back_own, axis=-1)
    probs_own = own_rows(router_probs.reshape(group_images, seq_len, experts))
    prob_grad = jnp.sum(gate_grad[..., None] * onehot_own, axis=2)
    logit_grad = probs_own * (prob_grad - jnp.sum(probs_own * prob_grad, axis=-1, keepdims=True))
    normed_grad = row_sum + jnp.einsum(
        "bpe,de->bpd", logit_grad, router_back.astype(jnp.float32), precision=PRECISE
    )
    router_grad = jnp.einsum(
        "bpd,bpe->de", normed_two.astype(jnp.float32), logit_grad, precision=PRECISE
    )
    back_bias_grad = jnp.einsum(
        "bpk,bpke,bpd->ed", gates_own, onehot_own, own_grad, precision=PRECISE
    )
    norm_two_pull = jax.vjp(layer_norm, state, gain_two_f, bias_two_f)[1]
    state_grad, gain_two_grad, bias_two_grad = norm_two_pull(normed_grad)
    state_grad = state_grad + own_grad
    proj_bias_grad = jnp.sum(state_grad, axis=(0, 1))
    fetched = fetch_attention()
    qkv_back, proj_back = (fetched[0], fetched[1])
    state_rows = lax.all_gather(state_grad.astype(jnp.bfloat16), "tensor", axis=0, tiled=True)
    proj_grad = jnp.einsum("bsf,bsd->fd", attended, state_rows, preferred_element_type=jnp.float32)
    attended_grad = jnp.einsum(
        "bsd,fd->bsf", state_rows, proj_back, preferred_element_type=jnp.float32
    )
    attended_grad = attended_grad.astype(jnp.bfloat16).reshape(
        group_images, seq_len, heads_local, HEAD_DIM
    )
    weights_again = jnp.exp(scores_of(query_heads, key_heads) - log_total)
    weight_grad = jnp.einsum(
        "bqhe,bkhe->bhqk", attended_grad, value_heads, preferred_element_type=jnp.float32
    )
    centre = jnp.sum(weights_again * weight_grad, axis=-1, keepdims=True)
    score_grad = (weights_again * (weight_grad - centre)).astype(jnp.bfloat16)
    query_grad = (
        jnp.einsum("bhqk,bkhe->bqhe", score_grad, key_heads, preferred_element_type=jnp.float32)
        * score_scale
    )
    key_grad = (
        jnp.einsum("bhqk,bqhe->bkhe", score_grad, query_heads, preferred_element_type=jnp.float32)
        * score_scale
    )
    value_grad = jnp.einsum(
        "bhqk,bqhe->bkhe",
        weights_again.astype(jnp.bfloat16),
        attended_grad,
        preferred_element_type=jnp.float32,
    )
    heads_grad = jnp.stack([query_grad, key_grad, value_grad], axis=2).astype(jnp.bfloat16)
    heads_grad = heads_grad.reshape(group_images, seq_len, 3, heads_local * HEAD_DIM)
    qkv_grad = jnp.einsum("bsd,bskf->dkf", rows_one, heads_grad, preferred_element_type=jnp.float32)
    rows_grad = jnp.einsum(
        "bskf,dkf->bsd", heads_grad, qkv_back, preferred_element_type=jnp.float32
    )
    normed_one_grad = lax.psum_scatter(rows_grad, "tensor", scatter_dimension=0, tiled=True)
    norm_one_pull = jax.vjp(layer_norm, source, gain_one_f, bias_one_f)[1]
    source_grad, gain_one_grad, bias_one_grad = norm_one_pull(normed_one_grad)
    input_grad = state_grad + source_grad
    qkv_part, proj_part = (
        lax.psum_scatter(qkv_grad, "dp", scatter_dimension=0, tiled=True),
        lax.psum_scatter(proj_grad, "dp", scatter_dimension=1, tiled=True),
    )
    hidden_cols = in_bias_grad.shape[1]
    bias_full = lax.dynamic_update_slice_in_dim(
        jnp.zeros((experts, hidden_cols * tensor_count), jnp.float32),
        in_bias_grad,
        tensor_rank * hidden_cols,
        1,
    )
    totals = lax.psum(
        (
            gain_one_grad,
            bias_one_grad,
            proj_bias_grad,
            gain_two_grad,
            bias_two_grad,
            router_grad,
            back_bias_grad,
            bias_full,
        ),
        ("dp", "tensor"),
    )
    share = model_width // dp_count

    def own_share(values, axis_dim):
        return lax.dynamic_slice_in_dim(values, dp_rank * share, share, axis_dim)

    bias_share = bias_full.shape[1] // (dp_count * tensor_count)
    in_bias_out = lax.dynamic_slice_in_dim(
        totals[7], (dp_rank * tensor_count + tensor_rank) * bias_share, bias_share, 1
    )
    return (
        block_out,
        input_grad,
        own_share(totals[0], 0),
        own_share(totals[1], 0),
        qkv_part,
        proj_part,
        own_share(totals[2], 0),
        own_share(totals[3], 0),
        own_share(totals[4], 0),
        own_share(totals[5], 0),
        in_part,
        in_bias_out,
        out_part,
        own_share(totals[6], 1),
    )


def solution(mesh):
    placed = (
        P(("dp", "tensor"), None, None),
        P("dp"),
        P("dp"),
        P("dp", None, "tensor"),
        P("tensor", "dp"),
        P("dp"),
        P("dp"),
        P("dp"),
        P("dp", None),
        P(None, "dp", "tensor"),
        P(None, "tensor"),
        P(None, "tensor", "dp"),
        P(None, "dp"),
        P("dp", None, None),
        P("dp", None, None),
        P(("dp", "tensor"), None, None),
    )
    return jax.shard_map(
        per_device,
        mesh=mesh,
        in_specs=placed,
        out_specs=(
            P(("dp", "tensor"), None, None),
            P(("dp", "tensor"), None, None),
            P("dp"),
            P("dp"),
            P("dp", None, "tensor"),
            P("tensor", "dp"),
            P("dp"),
            P("dp"),
            P("dp"),
            P("dp", None),
            P(None, "dp", "tensor"),
            P(None, ("dp", "tensor")),
            P(None, "tensor", "dp"),
            P(None, "dp"),
        ),
        check_vma=False,
    )
```

profile of v0, /device:TPU:0, one launch (start us, length us, event | category | flops | bytes accessed | tf_op | source)
XLA Modules:
  0.0 1171.3 jit_solution(6200482732531311500)
XLA Ops:
  13.3 38.8 %all-reduce.9 = (bf16[768]{0:T(1024)(128)(2,1)S(1)}, bf16[768]{0:T(1024)(128)(2,1)S(1)}, bf16[768]{0:T(1024)(128)(2,1)S(1)}, bf16[768]{0:T(1024)(128)(2,1)S(1)}, bf16[768]{0:T(1024)(128)(2,1)S(1)}) all-reduce(bf16[768]{0:T(1024)(128)(2,1)S(1)} %dynamic-update-slice.1, ...), channel_id=1, replica_groups=mesh['dp'=8,'tensor'=4] {'dp'}, use_global_device_ids=true, to_apply=%add.3 | all-reduce | flops 3840 | bytes 15360
  57.5 36.2 %all_gather.53 = bf16[768,3,192]{2,1,0:T(4,128)(2,1)S(1)} all-gather(bf16[96,3,192]{2,1,0:T(4,128)(2,1)S(1)} %copy.121), channel_id=1, replica_groups=mesh['dp'=8,'tensor'=4] {'dp'}, dimensions={0}, use_global_device_ids=true | all-gather | bytes 995328 | tf_op jit(solution)/shard_map/all_gather | solution.py:59
  94.8 31.0 %all_gather.54 = bf16[192,768]{0,1:T(8,128)(2,1)S(1)} all-gather(bf16[192,96]{0,1:T(8,128)(2,1)S(1)} %copy.127), channel_id=1, replica_groups=mesh['dp'=8,'tensor'=4] {'dp'}, dimensions={1}, use_global_device_ids=true | all-gather | bytes 331776 | tf_op jit(solution)/shard_map/all_gather | solution.py:60
  133.2 31.5 %reduce-scatter.11.cloned.1.call-done = f32[1,197,768]{2,1,0:T(8,128)} async-done(((f32[4,197,768]{2,1,0:T(8,128)}), f32[1,197,768]{2,1,0:T(8,128)}) %reduce-scatter.11.cloned.1.call-update) | async-done | bytes 605200 | tf_op jit(solution)/shard_map/reduce_scatter | solution.py:111
  169.5 20.5 %all-gather = bf16[8,96,4]{1,2,0:T(4,128)(2,1)S(1)} all-gather(bf16[1,96,4]{1,2,0:T(4,128)(2,1)S(1)} %bitcast.176), channel_id=1, replica_groups=mesh['dp'=8,'tensor'=4] {'dp'}, dimensions={0}, use_global_device_ids=true | all-gather | bytes 6912 | tf_op jit(solution)/shard_map/all_gather | solution.py:70
  190.2 8.8 scatter_custom_fusion
  204.5 7.5 mul.331
  213.9 6.3 gather_fusion
  228.6 6.3 gather_fusion.2
  238.9 46.7 %all-gather.13.cloned.1.call-done = bf16[4,768,768]{2,1,0:T(8,128)(2,1)} async-done(((bf16[4,96,768]{2,1,0:T(8,128)(2,1)}), bf16[4,768,768]{2,1,0:T(8,128)(2,1)}) %all-gather.13.cloned.1.call-update) | async-done | bytes 4718608 | tf_op jit(solution)/shard_map/all_gather | solution.py:68
  285.6 6.8 fusion.73
  292.4 73.5 %all-gather.15.cloned.1.call-done = bf16[4,768,768]{1,2,0:T(8,128)(2,1)} async-done(((bf16[4,768,96]{1,2,0:T(8,128)(2,1)}), bf16[4,768,768]{1,2,0:T(8,128)(2,1)}) %all-gather.15.cloned.1.call-update) | async-done | bytes 4718608 | tf_op jit(solution)/shard_map/all_gather | solution.py:69
  365.9 9.3 convert_reduce_fusion
  381.1 5.3 reshape.376
  386.4 10.1 gather_fusion.3
  396.4 6.9 reshape.377
  403.3 8.1 reduce_sum.246
  413.2 8.9 fusion.66
  427.4 10.5 gather_fusion.1
  437.9 7.1 reshape.371
  445.0 13.8 %multiply_reduce_fusion = (f32[788,2]{1,0:T(8,128)}, f32[788,768]{1,0:T(8,128)}) fusion(f32[788,2,768]{2,1,0:T(2,128)} %reshape.371, f32[788,768]{1,0:T(8,128)S(1)} %copy-done.7, f32[788,2]{1,0:T(8,128)} %copy-done.15), kind=kLoop, calls=%fused_computation.16 | loop fusion | flops 4234712 | bytes 9695552 | tf_op jit(solution)/shard_map/reduce_sum | solution.py:188
  462.4 17.6 %all-gather.1 = bf16[8,96,4]{1,2,0:T(4,128)(2,1)S(1)} all-gather(bf16[1,96,4]{1,2,0:T(4,128)(2,1)S(1)} %bitcast.177), channel_id=1, replica_groups=mesh['dp'=8,'tensor'=4] {'dp'}, dimensions={0}, use_global_device_ids=true | all-gather | bytes 6912 | tf_op jit(solution)/shard_map/all_gather | solution.py:71
  481.2 6.4 all-reduce.7
  499.2 17.8 %all-gather.19.cloned.1.call-done = bf16[4,197,768]{2,1,0:T(8,128)(2,1)} async-done(((bf16[1,197,768]{2,1,0:T(8,128)(2,1)}), bf16[4,197,768]{2,1,0:T(8,128)(2,1)}) %all-gather.19.cloned.1.call-update) | async-done | bytes 1210384 | tf_op jit(solution)/shard_map/all_gather | solution.py:219
  531.7 29.1 %reduce-scatter.17.cloned.1.call-done = f32[1,197,768]{2,1,0:T(8,128)} async-done(((f32[4,197,768]{2,1,0:T(8,128)}), f32[1,197,768]{2,1,0:T(8,128)}) %reduce-scatter.17.cloned.1.call-update) | async-done | bytes 605200 | tf_op jit(solution)/shard_map/reduce_scatter | solution.py:253
  571.7 8.9 fusion.65
  582.3 6.9 fusion.75
  589.2 37.4 %reduce-scatter.25.cloned.1.call-done = f32[96,192]{1,0:T(8,128)} async-done(((f32[768,192]{1,0:T(8,128)}), f32[96,192]{1,0:T(8,128)}) %reduce-scatter.25.cloned.1.call-update) | async-done | bytes 73744
  629.7 127.4 %all-reduce.12.cloned.1.call-done = (f32[768]{0:T(1024)}, f32[768]{0:T(1024)}, f32[768]{0:T(1024)}, f32[768]{0:T(1024)}, f32[768]{0:T(1024)}, /*index=5*/f32[768...) async-done(((f32[768]{0:T(1024)}, f32[768]{0:T(1024)}, f32[768]{0:T(1024)}, f32[768]{0:T(1024)}, f32[768]{0:T(1024)}, /*index=5*/f32[768,4]{0,1:T(4,128)}, f32[4,3072]{1,0:T(4,128)}, ...) | async-done | bytes 89104 | tf_op jit(solution)/shard_map/psum | solution.py:268
  766.1 65.0 %reduce-scatter.19.cloned.1.call-done = f32[96,3,192]{2,0,1:T(8,128)} async-done(((f32[768,3,192]{2,0,1:T(8,128)}), f32[96,3,192]{2,0,1:T(8,128)}) %reduce-scatter.19.cloned.1.call-update) | async-done | bytes 221200 | tf_op jit(solution)/shard_map/reduce_scatter | solution.py:258
  831.1 166.6 %reduce-scatter.23.cloned.1.call-done = f32[4,768,96]{1,2,0:T(8,128)} async-done(((f32[4,768,768]{1,2,0:T(8,128)}), f32[4,768,96]{1,2,0:T(8,128)}) %reduce-scatter.23.cloned.1.call-update) | async-done | bytes 1179664 | tf_op jit(solution)/shard_map/reduce_scatter | solution.py:182
  997.7 166.6 %reduce-scatter.21.cloned.1.call-done = f32[4,96,768]{2,1,0:T(8,128)} async-done(((f32[4,768,768]{2,1,0:T(8,128)}), f32[4,96,768]{2,1,0:T(8,128)}) %reduce-scatter.21.cloned.1.call-update) | async-done | bytes 1179664 | tf_op jit(solution)/shard_map/reduce_scatter | solution.py:181
  (264 shorter events, 111.6 us)
Async XLA Ops:
  7.2 118.6 %all-gather.9.cloned.1.call-start = ((), (), s32[]{:S(2)}) async-start(), calls=%async_computation.8 | async-start | bytes 1536000 | tf_op jit(solution)/shard_map/all_gather | solution.py:89
  54.5 40.1 %copy-start.45 = (f32[197]{0:T(256)}, f32[197]{0:T(256)S(1)}, u32[]{:S(2)}) copy-start(f32[197]{0:T(256)S(1)} %fusion.29) | copy-start | bytes 2368
  54.5 40.1 %copy-start.40 = (f32[197]{0:T(256)}, f32[197]{0:T(256)S(1)}, u32[]{:S(2)}) copy-start(f32[197]{0:T(256)S(1)} %fusion.56) | copy-start | bytes 2368
  56.4 38.2 %copy-start.34 = (bf16[192,96]{1,0:T(8,128)(2,1)S(1)}, bf16[192,96]{1,0:T(8,128)(2,1)}, u32[]{:S(2)}) copy-start(bf16[192,96]{1,0:T(8,128)(2,1)} %param.20) | copy-start | bytes 110596
  56.5 108.2 %reduce-scatter.11.cloned.1.call-start = ((), (), s32[]{:S(2)}) async-start(), calls=%async_computation.9 | async-start | bytes 3072000 | tf_op jit(solution)/shard_map/reduce_scatter | solution.py:111
  93.7 34.5 %copy-start.11 = (bf16[768,3,192]{2,1,0:T(4,128)(2,1)}, bf16[768,3,192]{2,1,0:T(4,128)(2,1)S(1)}, u32[]{:S(2)}) copy-start(bf16[768,3,192]{2,1,0:T(4,128)(2,1)S(1)} %all_gather.53) | copy-start | bytes 2654212
  130.3 34.4 %copy-start.8 = (bf16[1,197,768]{2,1,0:T(8,128)(2,1)S(1)}, bf16[1,197,768]{2,1,0:T(8,128)(2,1)}, u32[]{:S(2)}) copy-start(bf16[1,197,768]{2,1,0:T(8,128)(2,1)} %param.16) | copy-start | bytes 907780
  132.3 36.0 %copy-start.29 = (s32[4,197,2]{1,2,0:T(2,128)S(1)}, s32[4,197,2]{1,2,0:T(2,128)}, u32[]{:S(2)}) copy-start(s32[4,197,2]{1,2,0:T(2,128)} %param.29) | copy-start | bytes 18916
  132.4 36.0 %copy-start.51 = (s32[4,197,2]{1,2,0:T(2,128)S(1)}, s32[4,197,2]{1,2,0:T(2,128)}, u32[]{:S(2)}) copy-start(s32[4,197,2]{1,2,0:T(2,128)} %param.30) | copy-start | bytes 18916
  132.4 66.7 %all-gather.17.cloned.1.call-start = ((), (), s32[]{:S(2)}) async-start(), calls=%async_computation.14 | async-start | bytes 1536000 | tf_op jit(solution)/shard_map/all_gather | solution.py:160
  133.1 79.0 %all-gather.11.cloned.1.call-start = ((), (), s32[]{:S(2)}) async-start(), calls=%async_computation.10 | async-start | bytes 1536000 | tf_op jit(solution)/shard_map/all_gather | solution.py:117
  133.2 35.6 %copy-start.52 = (bf16[4,768]{1,0:T(4,128)(2,1)S(1)}, bf16[4,768]{1,0:T(4,128)(2,1)}, u32[]{:S(2)}) copy-start(bf16[4,768]{1,0:T(4,128)(2,1)} %param.26) | copy-start | bytes 18436
  133.2 36.2 %copy-start.53 = (bf16[96,4]{0,1:T(4,128)(2,1)S(1)}, bf16[96,4]{0,1:T(4,128)(2,1)}, u32[]{:S(2)}) copy-start(bf16[96,4]{0,1:T(4,128)(2,1)} %param.24) | copy-start | bytes 2308
  167.1 118.4 %all-gather.13.cloned.1.call-start = ((), (), s32[]{:S(2)}) async-start(), calls=%async_computation.11 | async-start | bytes 5308416 | tf_op jit(solution)/shard_map/all_gather | solution.py:68
  167.7 198.2 %all-gather.15.cloned.1.call-start = ((), (), s32[]{:S(2)}) async-start(), calls=%async_computation.12 | async-start | bytes 5308416 | tf_op jit(solution)/shard_map/all_gather | solution.py:69
  168.3 320.7 %reduce-scatter.15.cloned.1.call-start = ((), (), s32[]{:S(2)}) async-start(), calls=%async_computation.15 | async-start | bytes 3072000 | tf_op jit(solution)/shard_map/reduce_scatter | solution.py:190
  190.0 34.1 %copy-start.32 = (bf16[768,4]{0,1:T(4,128)(2,1)}, bf16[768,4]{0,1:T(4,128)(2,1)S(1)}, u32[]{:S(2)}) copy-start(bf16[768,4]{0,1:T(4,128)(2,1)S(1)} %reshape.444) | copy-start | bytes 18436
  234.8 50.7 %copy-start.2 = (bf16[4,415,768]{2,1,0:T(8,128)(2,1)S(1)}, bf16[4,415,768]{2,1,0:T(8,128)(2,1)}, u32[]{:S(2)}) copy-start(bf16[4,415,768]{2,1,0:T(8,128)(2,1)} %reshape.369) | copy-start | bytes 7649284
  413.2 81.1 %reduce-scatter.13.cloned.1.call-start = ((), (), s32[]{:S(2)}) async-start(), calls=%async_computation.13 | async-start | bytes 3072000 | tf_op jit(solution)/shard_map/reduce_scatter | solution.py:146
  462.3 29.1 %copy-start.48 = (f32[197]{0:T(256)S(1)}, f32[197]{0:T(256)}, u32[]{:S(2)}) copy-start(f32[197]{0:T(256)} %copy-done.47) | copy-start | bytes 2368
  462.3 54.7 %all-gather.19.cloned.1.call-start = ((), (), s32[]{:S(2)}) async-start(), calls=%async_computation.16 | async-start | bytes 1536000 | tf_op jit(solution)/shard_map/all_gather | solution.py:219
  499.1 61.7 %reduce-scatter.17.cloned.1.call-start = ((), (), s32[]{:S(2)}) async-start(), calls=%async_computation.17 | async-start | bytes 3072000 | tf_op jit(solution)/shard_map/reduce_scatter | solution.py:253
  527.0 35.7 %copy-start.46 = (f32[197]{0:T(256)S(1)}, f32[197]{0:T(256)}, u32[]{:S(2)}) copy-start(f32[197]{0:T(256)} %copy-done.45) | copy-start | bytes 2368
  527.1 35.7 %copy-start.41 = (f32[197]{0:T(256)S(1)}, f32[197]{0:T(256)}, u32[]{:S(2)}) copy-start(f32[197]{0:T(256)} %copy-done.40) | copy-start | bytes 2368
  527.1 99.6 %reduce-scatter.25.cloned.1.call-start = ((), (), s32[]{:S(2)}) async-start(), calls=%async_computation.21 | async-start | bytes 884736
  530.0 34.9 %copy-start.14 = (f32[1,197,768]{2,1,0:T(8,128)S(1)}, f32[1,197,768]{2,1,0:T(8,128)}, u32[]{:S(2)}) copy-start(f32[1,197,768]{2,1,0:T(8,128)} %copy-done.13) | copy-start | bytes 1815556
  530.0 34.9 %copy-start.50 = (f32[197]{0:T(256)S(1)}, f32[197]{0:T(256)}, u32[]{:S(2)}) copy-start(f32[197]{0:T(256)} %copy-done.49) | copy-start | bytes 2368
  531.6 225.5 %all-reduce.12.cloned.1.call-start = ((), (), s32[]{:S(2)}) async-start(), calls=%async_computation.22 | async-start | bytes 188416 | tf_op jit(solution)/shard_map/psum | solution.py:268
  531.7 35.1 %copy-start.28 = (f32[4,3072]{1,0:T(4,128)}, f32[4,3072]{1,0:T(4,128)S(1)}, u32[]{:S(2)}) copy-start(f32[4,3072]{1,0:T(4,128)S(1)} %constant_dynamic-update-slice_fusion) | copy-start | bytes 147460
  566.9 264.2 %reduce-scatter.19.cloned.1.call-start = ((), (), s32[]{:S(2)}) async-start(), calls=%async_computation.18 | async-start | bytes 2654208 | tf_op jit(solution)/shard_map/reduce_scatter | solution.py:258
  571.6 426.1 %reduce-scatter.23.cloned.1.call-start = ((), (), s32[]{:S(2)}) async-start(), calls=%async_computation.20 | async-start | bytes 10616832 | tf_op jit(solution)/shard_map/reduce_scatter | solution.py:182
  580.6 583.7 %reduce-scatter.21.cloned.1.call-start = ((), (), s32[]{:S(2)}) async-start(), calls=%async_computation.19 | async-start | bytes 10616832 | tf_op jit(solution)/shard_map/reduce_scatter | solution.py:181
  (39 other events, 302.6 us)
Sparse Core Ops, SparseCore 0:
  56.6 14.9 all-gather.8
  132.5 32.1 reduce-scatter.10
  166.3 17.7 all-gather.16
  185.6 17.7 all-gather.10
  205.6 79.8 all-gather.12
  287.8 78.0 all-gather.14
  413.3 31.7 reduce-scatter.14
  462.4 31.7 reduce-scatter.12
  499.2 17.7 all-gather.18
  527.2 33.6 reduce-scatter.16
  564.2 62.4 reduce-scatter.24
  634.1 123.0 all-reduce.11
  761.2 69.8 reduce-scatter.18
  835.1 162.4 reduce-scatter.22
  1001.7 162.5 reduce-scatter.20
where the time goes:
time: 1180 us; the launch traced here: 1170 us
  waiting for transfers between devices  766 us (65%)
  blocking collectives  151 us (13%)
  local copies, waits for them, and re-layouts  122 us (10%)
  matrix products  70.2 us (6%)
  other arithmetic  44.7 us (4%)
  between operations  16 us (1%)
    reduce_scatter x1, waiting for transfers between devices, per_device(): lax.psum_scatter(in_grad, 'dp', scatter_dimension=1, tiled=True)  167 us
    reduce_scatter x1, waiting for transfers between devices, per_device(): lax.psum_scatter(out_grad, 'dp', scatter_dimension=2, tiled=True)  167 us
    psum x1, waiting for transfers between devices, per_device(): lax.psum((gain_one_grad, bias_one_grad, proj_bias_grad, gain_two_grad, bi...  127 us
    all_gather x1, waiting for transfers between devices, fetch_experts(): lax.all_gather(expert_out, 'dp', axis=2, tiled=True)  73.5 us
    reduce_scatter x1, waiting for transfers between devices, per_device(): lax.psum_scatter(qkv_grad, 'dp', scatter_dimension=0, tiled=True)  65 us
    all_gather x1, waiting for transfers between devices, fetch_experts(): lax.all_gather(expert_in, 'dp', axis=1, tiled=True)  46.7 us
    unnamed x2, blocking collectives  45.3 us
    unnamed x16, waiting for transfers between devices  39.3 us
  transfers between devices with their start and end apart: 15, of which 11 were waited for; matrix products, arithmetic and copies ran while one was open for 13% of the time, Pallas kernels for 0%

commit v1 on v0

v1 whole, which is shorter than its diff:
```python
import jax
import jax.numpy as jnp
from jax import lax
from jax.sharding import PartitionSpec as P

HEAD_DIM = 64
SEQ = 197


EPSILON = 1e-06
PRECISE = lax.Precision.HIGHEST


def layer_norm(values, gain, bias):
    centred = values - jnp.mean(values, axis=-1, keepdims=True)
    spread = jnp.mean(centred * centred, axis=-1, keepdims=True)
    return centred * lax.rsqrt(spread + EPSILON) * gain + bias


def gelu_tanh(values):
    return jax.nn.gelu(values, approximate=True)


def per_device(
    inputs,
    ln1_gain,
    ln1_bias,
    qkv_weight,
    proj_weight,
    proj_bias,
    ln2_gain,
    ln2_bias,
    router_weight,
    expert_in,
    expert_in_bias,
    expert_out,
    expert_out_bias,
    expert_ids,
    slot_ids,
    cotangent,
):
    local_images, seq_len, model_width = inputs.shape
    tensor_count = lax.axis_size("tensor")
    dp_count = lax.axis_size("dp")
    tensor_rank = lax.axis_index("tensor")
    dp_rank = lax.axis_index("dp")
    group_images = local_images * tensor_count
    experts = expert_in.shape[0]
    tokens = group_images * SEQ
    slot_count = 40 * tokens // (19 * experts) + 1
    slot_rows = -(-slot_count // 16) * 16
    heads_local = qkv_weight.shape[2] // HEAD_DIM
    score_scale = HEAD_DIM ** (-0.5)

    def own_rows(values):
        return lax.dynamic_slice_in_dim(values, tensor_rank * local_images, local_images, 0)

    def scatter_rows(values):
        return lax.psum_scatter(
            values.astype(jnp.bfloat16), "tensor", scatter_dimension=0, tiled=True
        ).astype(jnp.float32)

    def split_three(values):
        first = values.astype(jnp.bfloat16)
        rest = values - first.astype(jnp.float32)
        second = rest.astype(jnp.bfloat16)
        third = (rest - second.astype(jnp.float32)).astype(jnp.bfloat16)
        return jnp.concatenate([first, second, third], axis=-1)

    def fetch_attention():
        return (
            lax.all_gather(qkv_weight, "dp", axis=0, tiled=True),
            lax.all_gather(proj_weight, "dp", axis=1, tiled=True),
            lax.all_gather(ln1_gain, "dp", axis=0, tiled=True),
            lax.all_gather(ln1_bias, "dp", axis=0, tiled=True),
            lax.all_gather(proj_bias, "dp", axis=0, tiled=True),
        )

    def fetch_experts():
        return (
            lax.all_gather(expert_in, "dp", axis=1, tiled=True),
            lax.all_gather(expert_out, "dp", axis=2, tiled=True),
            lax.all_gather(router_weight, "dp", axis=0, tiled=True),
            lax.all_gather(expert_out_bias, "dp", axis=1, tiled=True),
            lax.all_gather(ln2_gain, "dp", axis=0, tiled=True),
            lax.all_gather(ln2_bias, "dp", axis=0, tiled=True),
        )

    def scores_of(query_heads, key_heads):
        return (
            jnp.einsum(
                "bqhe,bkhe->bhqk", query_heads, key_heads, preferred_element_type=jnp.float32
            )
            * score_scale
        )

    qkv_full, proj_full, gain_one, bias_one, proj_shift = fetch_attention()
    gain_one_f = gain_one.astype(jnp.float32)
    bias_one_f = bias_one.astype(jnp.float32)
    source = inputs.astype(jnp.float32)
    normed_one = layer_norm(source, gain_one_f, bias_one_f).astype(jnp.bfloat16)
    rows_one = lax.all_gather(normed_one, "tensor", axis=0, tiled=True)
    mixed = jnp.einsum(
        "bsd,dkf->bskf", rows_one, qkv_full, preferred_element_type=jnp.float32
    ).astype(jnp.bfloat16)
    head_blocks = mixed.reshape(group_images, seq_len, 3, heads_local, HEAD_DIM)
    query_heads = head_blocks[:, :, 0]
    key_heads = head_blocks[:, :, 1]
    value_heads = head_blocks[:, :, 2]
    scores = scores_of(query_heads, key_heads)
    top_score = jnp.max(scores, axis=-1, keepdims=True)
    raised = jnp.exp(scores - top_score)
    row_total = jnp.sum(raised, axis=-1, keepdims=True)
    weights = raised / row_total
    log_total = top_score + jnp.log(row_total)
    attended = jnp.einsum(
        "bhqk,bkhe->bqhe",
        weights.astype(jnp.bfloat16),
        value_heads,
        preferred_element_type=jnp.float32,
    )
    attended = attended.astype(jnp.bfloat16).reshape(group_images, seq_len, heads_local * HEAD_DIM)
    attn_terms = jnp.einsum("bsf,fd->bsd", attended, proj_full, preferred_element_type=jnp.float32)
    attn_sum = scatter_rows(attn_terms)
    state = source + attn_sum + proj_shift.astype(jnp.float32)
    in_full, out_full, router_full, back_shift, gain_two, bias_two = fetch_experts()
    gain_two_f = gain_two.astype(jnp.float32)
    bias_two_f = bias_two.astype(jnp.float32)
    normed_two = layer_norm(state, gain_two_f, bias_two_f).astype(jnp.bfloat16)
    rows_two = lax.all_gather(normed_two, "tensor", axis=0, tiled=True)
    out_rows = lax.all_gather(cotangent, "tensor", axis=0, tiled=True)
    token_rows = rows_two.reshape(tokens, model_width)
    grad_rows = out_rows.reshape(tokens, model_width)
    choice_ids = expert_ids.reshape(tokens, 2)
    places = choice_ids * slot_rows + slot_ids.reshape(tokens, 2)
    slot_index = jnp.arange(experts * slot_rows, dtype=jnp.int32)[:, None]
    chosen = (
        (slot_index == places[:, 0][None, :]) | (slot_index == places[:, 1][None, :])
    ).astype(jnp.bfloat16)
    logits = jnp.dot(token_rows, router_full, preferred_element_type=jnp.float32)
    router_probs = jax.nn.softmax(logits, axis=-1)
    expert_mask = (
        jnp.arange(experts * slot_rows)[:, None] // slot_rows == jnp.arange(experts)[None, :]
    )
    slot_probs = jnp.dot(chosen, split_three(router_probs), preferred_element_type=jnp.float32)
    slot_gates = jnp.sum(
        jnp.where(expert_mask[:, None, :], slot_probs.reshape(-1, 3, experts), 0.0), axis=(1, 2)
    )
    dispatched = (
        jnp.dot(chosen, token_rows, preferred_element_type=jnp.float32)
        .astype(jnp.bfloat16)
        .reshape(experts, slot_rows, model_width)
    )
    slot_out = (
        jnp.dot(chosen, grad_rows, preferred_element_type=jnp.float32)
    )
    slot_grad = (
        (slot_gates[:, None] * slot_out)
        .astype(jnp.bfloat16)
        .reshape(experts, slot_rows, model_width)
    )
    pre = (
        jnp.einsum("ecd,edf->ecf", dispatched, in_full, preferred_element_type=jnp.float32)
        + expert_in_bias.astype(jnp.float32)[:, None, :]
    )
    hidden = gelu_tanh(pre).astype(jnp.bfloat16)
    expert_terms = jnp.einsum(
        "ecf,efd->ecd", hidden, out_full, preferred_element_type=jnp.float32
    ).reshape(experts * slot_rows, model_width)
    gated_terms = (slot_gates[:, None] * expert_terms).astype(jnp.bfloat16)
    slot_dgate = jnp.sum(expert_terms * slot_out, axis=-1)
    mixed_terms = jnp.einsum(
        "st,sd->td", chosen, gated_terms, preferred_element_type=jnp.float32
    )
    mixed_sum = scatter_rows(mixed_terms.reshape(group_images, seq_len, model_width))
    own_ids = own_rows(expert_ids.reshape(group_images, seq_len, 2))
    onehot_own = (own_ids[..., None] == jnp.arange(experts)).astype(jnp.float32)
    probs_own = own_rows(router_probs.reshape(group_images, seq_len, experts))
    probs_chosen = probs_own * jnp.sum(onehot_own, axis=2)
    back_f = back_shift.astype(jnp.float32)
    shift_own = jnp.einsum("bpe,ed->bpd", probs_chosen, back_f, precision=PRECISE)
    result = state + mixed_sum + shift_own
    block_out = result.astype(jnp.bfloat16)
    own_grad = cotangent.astype(jnp.float32)
    out_grad = jnp.einsum("ecf,ecd->efd", hidden, slot_grad, preferred_element_type=jnp.float32)
    out_part = lax.psum_scatter(
        out_grad.astype(jnp.bfloat16), "dp", scatter_dimension=2, tiled=True
    ).astype(jnp.float32)
    hidden_grad = jnp.einsum(
        "ecd,efd->ecf", slot_grad, out_full, preferred_element_type=jnp.float32
    )
    gelu_pull = jax.vjp(gelu_tanh, pre)[1]
    pre_grad = gelu_pull(hidden_grad)[0].astype(jnp.bfloat16)
    in_grad = jnp.einsum("ecd,ecf->edf", dispatched, pre_grad, preferred_element_type=jnp.float32)
    in_bias_grad = jnp.sum(pre_grad.astype(jnp.float32), axis=1)
    in_part = lax.psum_scatter(
        in_grad.astype(jnp.bfloat16), "dp", scatter_dimension=1, tiled=True
    ).astype(jnp.float32)
    slot_back = (
        jnp.einsum("ecf,edf->ecd", pre_grad, in_full, preferred_element_type=jnp.float32)
        .astype(jnp.bfloat16)
        .reshape(experts * slot_rows, model_width)
    )
    row_back = jnp.einsum("st,sd->td", chosen, slot_back, preferred_element_type=jnp.float32)
    dgate_cols = split_three(jnp.where(expert_mask, slot_dgate[:, None], 0.0))
    prob_parts = jnp.sum(
        jnp.einsum("st,sk->tk", chosen, dgate_cols, preferred_element_type=jnp.float32).reshape(
            tokens, 3, experts
        ),
        axis=1,
    )
    row_sum = scatter_rows(row_back.reshape(group_images, seq_len, model_width))
    prob_sum = lax.psum_scatter(
        prob_parts.reshape(group_images, seq_len, experts),
        "tensor",
        scatter_dimension=0,
        tiled=True,
    )
    prob_grad = prob_sum + jnp.sum(onehot_own, axis=2) * jnp.einsum(
        "bpd,ed->bpe", own_grad, back_f, precision=PRECISE
    )
    logit_grad = probs_own * (prob_grad - jnp.sum(probs_own * prob_grad, axis=-1, keepdims=True))
    normed_grad = row_sum + jnp.einsum(
        "bpe,de->bpd", logit_grad, router_full.astype(jnp.float32), precision=PRECISE
    )
    router_grad = jnp.einsum(
        "bpd,bpe->de", normed_two.astype(jnp.float32), logit_grad, precision=PRECISE
    )
    back_bias_grad = jnp.einsum("bpe,bpd->ed", probs_chosen, own_grad, precision=PRECISE)
    norm_two_pull = jax.vjp(layer_norm, state, gain_two_f, bias_two_f)[1]
    state_grad, gain_two_grad, bias_two_grad = norm_two_pull(normed_grad)
    state_grad = state_grad + own_grad
    proj_bias_grad = jnp.sum(state_grad, axis=(0, 1))
    state_rows = lax.all_gather(state_grad.astype(jnp.bfloat16), "tensor", axis=0, tiled=True)
    proj_grad = jnp.einsum("bsf,bsd->fd", attended, state_rows, preferred_element_type=jnp.float32)
    attended_grad = jnp.einsum(
        "bsd,fd->bsf", state_rows, proj_full, preferred_element_type=jnp.float32
    )
    attended_grad = attended_grad.astype(jnp.bfloat16).reshape(
        group_images, seq_len, heads_local, HEAD_DIM
    )
    weight_grad = jnp.einsum(
        "bqhe,bkhe->bhqk", attended_grad, value_heads, preferred_element_type=jnp.float32
    )
    centre = jnp.sum(weights * weight_grad, axis=-1, keepdims=True)
    score_grad = (weights * (weight_grad - centre)).astype(jnp.bfloat16)
    query_grad = (
        jnp.einsum("bhqk,bkhe->bqhe", score_grad, key_heads, preferred_element_type=jnp.float32)
        * score_scale
    )
    key_grad = (
        jnp.einsum("bhqk,bqhe->bkhe", score_grad, query_heads, preferred_element_type=jnp.float32)
        * score_scale
    )
    value_grad = jnp.einsum(
        "bhqk,bqhe->bkhe",
        weights.astype(jnp.bfloat16),
        attended_grad,
        preferred_element_type=jnp.float32,
    )
    heads_grad = jnp.stack([query_grad, key_grad, value_grad], axis=2).astype(jnp.bfloat16)
    heads_grad = heads_grad.reshape(group_images, seq_len, 3, heads_local * HEAD_DIM)
    qkv_grad = jnp.einsum("bsd,bskf->dkf", rows_one, heads_grad, preferred_element_type=jnp.float32)
    rows_grad = jnp.einsum(
        "bskf,dkf->bsd", heads_grad, qkv_full, preferred_element_type=jnp.float32
    )
    normed_one_grad = scatter_rows(rows_grad)
    norm_one_pull = jax.vjp(layer_norm, source, gain_one_f, bias_one_f)[1]
    source_grad, gain_one_grad, bias_one_grad = norm_one_pull(normed_one_grad)
    input_grad = state_grad + source_grad
    qkv_part = lax.psum_scatter(
        qkv_grad.astype(jnp.bfloat16), "dp", scatter_dimension=0, tiled=True
    ).astype(jnp.float32)
    proj_part = lax.psum_scatter(
        proj_grad.astype(jnp.bfloat16), "dp", scatter_dimension=1, tiled=True
    ).astype(jnp.float32)
    share = model_width // dp_count
    hidden_cols = in_bias_grad.shape[1]
    bias_share = hidden_cols // dp_count
    bias_full = lax.dynamic_update_slice_in_dim(
        jnp.zeros((experts, hidden_cols * tensor_count), jnp.float32),
        in_bias_grad,
        tensor_rank * hidden_cols,
        1,
    )
    packed = jnp.concatenate(
        [
            gain_one_grad.reshape(dp_count, share),
            bias_one_grad.reshape(dp_count, share),
            proj_bias_grad.reshape(dp_count, share),
            gain_two_grad.reshape(dp_count, share),
            bias_two_grad.reshape(dp_count, share),
            router_grad.reshape(dp_count, share * experts),
            back_bias_grad.reshape(experts, dp_count, share).transpose(1, 0, 2).reshape(dp_count, -1),
            bias_full.reshape(experts, dp_count, -1).transpose(1, 0, 2).reshape(dp_count, -1),
        ],
        axis=1,
    )
    totals = lax.psum(
        lax.psum_scatter(packed, "dp", scatter_dimension=0, tiled=True).reshape(-1), "tensor"
    )
    cuts = []
    at = 0
    for width in (share,) * 5 + (share * experts,) * 2:
        cuts.append(totals[at : at + width])
        at += width
    in_bias_out = lax.dynamic_slice_in_dim(
        totals[at:].reshape(experts, tensor_count * bias_share), tensor_rank * bias_share, bias_share, 1
    )
    return (
        block_out,
        input_grad,
        cuts[0],
        cuts[1],
        qkv_part,
        proj_part,
        cuts[2],
        cuts[3],
        cuts[4],
        cuts[5].reshape(share, experts),
        in_part,
        in_bias_out,
        out_part,
        cuts[6].reshape(experts, share),
    )


def solution(mesh):
    placed = (
        P(("dp", "tensor"), None, None),
        P("dp"),
        P("dp"),
        P("dp", None, "tensor"),
        P("tensor", "dp"),
        P("dp"),
        P("dp"),
        P("dp"),
        P("dp", None),
        P(None, "dp", "tensor"),
        P(None, "tensor"),
        P(None, "tensor", "dp"),
        P(None, "dp"),
        P("dp", None, None),
        P("dp", None, None),
        P(("dp", "tensor"), None, None),
    )
    return jax.shard_map(
        per_device,
        mesh=mesh,
        in_specs=placed,
        out_specs=(
            P(("dp", "tensor"), None, None),
            P(("dp", "tensor"), None, None),
            P("dp"),
            P("dp"),
            P("dp", None, "tensor"),
            P("tensor", "dp"),
            P("dp"),
            P("dp"),
            P("dp"),
            P("dp", None),
            P(None, "dp", "tensor"),
            P(None, ("dp", "tensor")),
            P(None, "tensor", "dp"),
            P(None, "dp"),
        ),
        check_vma=False,
    )
```

time: 1180 us -> 924 us (0.78)
  waiting for transfers between devices: 766 us -> 586 us
  local copies, waits for them, and re-layouts: 122 us -> 30.8 us
  matrix products: 70.2 us -> 85.1 us
  blocking collectives: 151 us -> 164 us
  other arithmetic: 44.7 us -> 32 us
    reduce_scatter x7, waiting for transfers between devices: 462 us -> 288 us  [the longest x1 96.9 us: per_device(): lax.psum_scatter(in_grad.astype(jnp.bfloat16), 'dp', scatter_dimension=1,...]
    psum x1 -> x0, waiting for transfers between devices: 127 us -> none  [per_device(): lax.psum((gain_one_grad, bias_one_grad, proj_bias_grad, gain_two_grad, bi...]
    unnamed x16 -> x17, waiting for transfers between devices: 39.3 us -> 134 us
    gather x4 -> x0, local copies, waits for them, and re-layouts: 33.2 us -> none  [the longest x1 10.5 us: per_device(): picked = expert_terms[places_flat].reshape(tokens, 2, model_width)]
    reshape x11 -> x15, local copies, waits for them, and re-layouts: 37.9 us -> 5.8 us  [the longest x1 2.67 us: per_device(): grad_rows = out_rows.reshape(tokens, model_width)]
    all_gather x1, waiting for transfers between devices: 46.7 us -> 71.8 us  [fetch_experts(): lax.all_gather(expert_in, 'dp', axis=1, tiled=True)]
    reduce_sum x6 -> x2, other arithmetic: 22.5 us -> 0.03 us  [the longest x1 0.02 us: per_device(): jnp.sum(jnp.einsum('st,sk->tk', chosen, dgate_cols, preferred_element_typ...]
    dot_general x8 -> x15, matrix products: 22.7 us -> 39.7 us  [the longest x1 5.95 us: per_device(): jnp.einsum('ecd,efd->ecf', slot_grad, out_full, preferred_element_type=jn...]
  transfers between devices with their start and end apart: 15 -> 15, of which waited for: 11 -> 12; matrix products, arithmetic and copies ran while one was open for 13% -> 9% of each run, Pallas kernels for 0% -> 0%
where the time goes in v1:
time: 924 us; the launch traced here: 915 us
  waiting for transfers between devices  586 us (63%)
  blocking collectives  164 us (18%)
  matrix products  85.1 us (9%)
  other arithmetic  32 us (3%)
  local copies, waits for them, and re-layouts  30.8 us (3%)
  between operations  15.7 us (2%)
    unnamed x17, waiting for transfers between devices  134 us
    reduce_scatter x1, waiting for transfers between devices, per_device(): lax.psum_scatter(in_grad.astype(jnp.bfloat16), 'dp', scatter_dimension=1,...  96.9 us
    reduce_scatter x1, waiting for transfers between devices, per_device(): lax.psum_scatter(out_grad.astype(jnp.bfloat16), 'dp', scatter_dimension=2...  83.4 us
    all_gather x1, waiting for transfers between devices, fetch_experts(): lax.all_gather(expert_out, 'dp', axis=2, tiled=True)  72.8 us
    all_gather x1, waiting for transfers between devices, fetch_experts(): lax.all_gather(expert_in, 'dp', axis=1, tiled=True)  71.8 us
    reduce_scatter x1, waiting for transfers between devices, per_device(): lax.psum_scatter(qkv_grad.astype(jnp.bfloat16), 'dp', scatter_dimension=0...  65.3 us
    unnamed x2, blocking collectives  49 us
    reduce_scatter x4, waiting for transfers between devices, scatter_rows(): lax.psum_scatter(values.astype(jnp.bfloat16), 'tensor', scatter_dimension...  42.3 us
  transfers between devices with their start and end apart: 15, of which 12 were waited for; matrix products, arithmetic and copies ran while one was open for 9% of the time, Pallas kernels for 0%

profile of v1, /device:TPU:0, one launch (start us, length us, event | category | flops | bytes accessed | tf_op | source)
XLA Modules:
  0.0 915.1 jit_solution(835375714835017363)
XLA Ops:
  13.4 38.8 %all-reduce.7 = (bf16[768]{0:T(1024)(128)(2,1)S(1)}, bf16[768]{0:T(1024)(128)(2,1)S(1)}, bf16[768]{0:T(1024)(128)(2,1)S(1)}, bf16[768]{0:T(1024)(128)(2,1)S(1)}, bf16[768]{0:T(1024)(128)(2,1)S(1)}) all-reduce(bf16[768]{0:T(1024)(128)(2,1)S(1)} %dynamic-update-slice.4, ...), channel_id=1, replica_groups=mesh['dp'=8,'tensor'=4] {'dp'}, use_global_device_ids=true, to_apply=%add.4 | all-reduce | flops 3840 | bytes 15360
  57.6 36.2 %all_gather.48 = bf16[768,3,192]{2,1,0:T(4,128)(2,1)S(1)} all-gather(bf16[96,3,192]{2,1,0:T(4,128)(2,1)S(1)} %copy.123), channel_id=1, replica_groups=mesh['dp'=8,'tensor'=4] {'dp'}, dimensions={0}, use_global_device_ids=true | all-gather | bytes 995328 | tf_op jit(solution)/shard_map/all_gather | solution.py:72
  94.8 31.0 %all_gather.49 = bf16[192,768]{0,1:T(8,128)(2,1)S(1)} all-gather(bf16[192,96]{0,1:T(8,128)(2,1)S(1)} %copy.129), channel_id=1, replica_groups=mesh['dp'=8,'tensor'=4] {'dp'}, dimensions={1}, use_global_device_ids=true | all-gather | bytes 331776 | tf_op jit(solution)/shard_map/all_gather | solution.py:73
  134.8 23.9 %reduce-scatter.11.cloned.1.call-done = bf16[1,197,768]{2,1,0:T(8,128)(2,1)} async-done(((bf16[4,197,768]{2,1,0:T(8,128)(2,1)}), bf16[1,197,768]{2,1,0:T(8,128)(2,1)}) %reduce-scatter.11.cloned.1.call-update) | async-done | bytes 302608 | tf_op jit(solution)/shard_map/reduce_scatter | solution.py:59
  164.2 20.5 %all-gather = bf16[8,96,4]{1,2,0:T(4,128)(2,1)S(1)} all-gather(bf16[1,96,4]{1,2,0:T(4,128)(2,1)S(1)} %bitcast.223), channel_id=1, replica_groups=mesh['dp'=8,'tensor'=4] {'dp'}, dimensions={0}, use_global_device_ids=true | all-gather | bytes 6912 | tf_op jit(solution)/shard_map/all_gather | solution.py:83
  187.5 3.3 or.18
  193.5 4.4 all-gather.11.cloned.1.call-done
  202.4 5.9 convolution_convert_fusion
  208.3 71.8 %all-gather.13.cloned.1.call-done = bf16[4,768,768]{2,1,0:T(8,128)(2,1)} async-done(((bf16[4,96,768]{2,1,0:T(8,128)(2,1)}), bf16[4,768,768]{2,1,0:T(8,128)(2,1)}) %all-gather.13.cloned.1.call-update) | async-done | bytes 4718608 | tf_op jit(solution)/shard_map/all_gather | solution.py:81
  280.1 7.5 fusion.101
  287.7 72.8 %all-gather.15.cloned.1.call-done = bf16[4,768,768]{1,2,0:T(8,128)(2,1)} async-done(((bf16[4,768,96]{1,2,0:T(8,128)(2,1)}), bf16[4,768,768]{1,2,0:T(8,128)(2,1)}) %all-gather.15.cloned.1.call-update) | async-done | bytes 4718608 | tf_op jit(solution)/shard_map/all_gather | solution.py:82
  360.5 6.5 fusion.91
  367.0 5.9 fusion.10
  374.5 3.4 multiply_convert_fusion
  378.5 5.9 convert_reduce_fusion
  386.8 3.5 convolution_convert_fusion.4
  390.3 17.7 %all-gather.1 = bf16[8,96,4]{1,2,0:T(4,128)(2,1)S(1)} all-gather(bf16[1,96,4]{1,2,0:T(4,128)(2,1)S(1)} %bitcast.224), channel_id=1, replica_groups=mesh['dp'=8,'tensor'=4] {'dp'}, dimensions={0}, use_global_device_ids=true | all-gather | bytes 6912 | tf_op jit(solution)/shard_map/all_gather | solution.py:84
  410.3 10.1 %all-reduce.5 = f32[4,197,4]{1,2,0:T(4,128)S(1)} all-reduce(f32[4,197,4]{1,2,0:T(4,128)S(1)} %copy.135), channel_id=5, replica_groups=mesh['dp'=8,'tensor'=4] {'tensor'}, use_global_device_ids=true, to_apply=%region_15.16.clone | all-reduce | flops 3152 | bytes 25216
  425.3 15.5 %all-gather.19.cloned.1.call-done = bf16[4,197,768]{2,1,0:T(8,128)(2,1)} async-done(((bf16[1,197,768]{2,1,0:T(8,128)(2,1)}), bf16[4,197,768]{2,1,0:T(8,128)(2,1)}) %all-gather.19.cloned.1.call-update) | async-done | bytes 1210384 | tf_op jit(solution)/shard_map/all_gather | solution.py:234
  450.9 2.9 multiply_convert_fusion.1
  453.8 3.5 convolution_convert_fusion.5
  460.4 3.8 bitcast_convert_fusion.1
  466.0 10.8 %reduce-scatter.17.cloned.1.call-done = bf16[1,197,768]{2,1,0:T(8,128)(2,1)} async-done(((bf16[4,197,768]{2,1,0:T(8,128)(2,1)}), bf16[1,197,768]{2,1,0:T(8,128)(2,1)}) %reduce-scatter.17.cloned.1.call-update) | async-done | bytes 302608 | tf_op jit(solution)/shard_map/reduce_scatter | solution.py:59
  481.8 8.5 convolution_convert_fusion.1
  490.6 7.3 convolution_convert_fusion.2
  497.9 7.6 reduce-scatter.13.cloned.1.call-done
  507.6 62.4 %reduce-scatter.25.cloned.1.call-done = bf16[96,192]{1,0:T(8,128)(2,1)} async-done(((bf16[768,192]{1,0:T(8,128)(2,1)}), bf16[96,192]{1,0:T(8,128)(2,1)}) %reduce-scatter.25.cloned.1.call-update) | async-done | bytes 36880
  571.6 65.3 %reduce-scatter.19.cloned.1.call-done = bf16[96,3,192]{2,0,1:T(8,128)(2,1)} async-done(((bf16[768,3,192]{2,0,1:T(8,128)(2,1)}), bf16[96,3,192]{2,0,1:T(8,128)(2,1)}) %reduce-scatter.19.cloned.1.call-update) | async-done | bytes 110608 | tf_op jit(solution)/shard_map/reduce_scatter | solution.py:271
  640.0 69.2 %all-reduce.10.cloned.1.call-done = f32[8,2784]{1,0:T(8,128)} async-done(((f32[8,2784]{1,0:T(8,128)}), f32[8,2784]{1,0:T(8,128)}) %all-reduce.10.cloned.1.call-update) | async-done | bytes 89104
  710.8 10.1 %psum.7 = f32[2784]{0:T(1024)S(1)} all-reduce(f32[2784]{0:T(1024)S(1)} %dynamic-slice_reduce_fusion), channel_id=1, replica_groups=mesh['dp'=8,'tensor'=4] {'tensor'}, use_global_device_ids=true, to_apply=%region_30.31 | all-reduce | flops 2784 | bytes 22272 | tf_op jit(solution)/shard_map/psum | solution.py:299
  723.7 83.4 %reduce-scatter.23.cloned.1.call-done = bf16[4,768,96]{1,2,0:T(8,128)(2,1)} async-done(((bf16[4,768,768]{1,2,0:T(8,128)(2,1)}), bf16[4,768,96]{1,2,0:T(8,128)(2,1)}) %reduce-scatter.23.cloned.1.call-update) | async-done | bytes 589840 | tf_op jit(solution)/shard_map/reduce_scatter | solution.py:186
  809.3 96.9 %reduce-scatter.21.cloned.1.call-done = bf16[4,96,768]{2,1,0:T(8,128)(2,1)} async-done(((bf16[4,768,768]{2,1,0:T(8,128)(2,1)}), bf16[4,96,768]{2,1,0:T(8,128)(2,1)}) %reduce-scatter.21.cloned.1.call-update) | async-done | bytes 589840 | tf_op jit(solution)/shard_map/reduce_scatter | solution.py:196
  (245 shorter events, 83.0 us)
Async XLA Ops:
  7.2 118.7 %all-gather.9.cloned.1.call-start = ((), (), s32[]{:S(2)}) async-start(), calls=%async_computation.8 | async-start | bytes 1536000 | tf_op jit(solution)/shard_map/all_gather | solution.py:102
  54.6 40.1 %copy-start.29 = (f32[197]{0:T(256)}, f32[197]{0:T(256)S(1)}, u32[]{:S(2)}) copy-start(f32[197]{0:T(256)S(1)} %fusion.45) | copy-start | bytes 2368
  56.5 38.2 %copy-start.22 = (bf16[192,96]{1,0:T(8,128)(2,1)S(1)}, bf16[192,96]{1,0:T(8,128)(2,1)}, u32[]{:S(2)}) copy-start(bf16[192,96]{1,0:T(8,128)(2,1)} %param.20) | copy-start | bytes 110596
  56.5 102.2 %reduce-scatter.11.cloned.1.call-start = ((), (), s32[]{:S(2)}) async-start(), calls=%async_computation.9 | async-start | bytes 1536000 | tf_op jit(solution)/shard_map/reduce_scatter | solution.py:59
  93.8 34.6 %copy-start.3 = (bf16[768,3,192]{2,1,0:T(4,128)(2,1)}, bf16[768,3,192]{2,1,0:T(4,128)(2,1)S(1)}, u32[]{:S(2)}) copy-start(bf16[768,3,192]{2,1,0:T(4,128)(2,1)S(1)} %all_gather.48) | copy-start | bytes 2654212
  131.5 27.2 %copy-start = (bf16[1,197,768]{2,1,0:T(8,128)(2,1)S(1)}, bf16[1,197,768]{2,1,0:T(8,128)(2,1)}, u32[]{:S(2)}) copy-start(bf16[1,197,768]{2,1,0:T(8,128)(2,1)} %param.16) | copy-start | bytes 907780
  133.9 30.3 %copy-start.35 = (bf16[96,4]{0,1:T(4,128)(2,1)S(1)}, bf16[96,4]{0,1:T(4,128)(2,1)}, u32[]{:S(2)}) copy-start(bf16[96,4]{0,1:T(4,128)(2,1)} %param.24) | copy-start | bytes 2308
  133.9 50.9 %copy-start.23 = (s32[4,197,2]{1,2,0:T(2,128)S(1)}, s32[4,197,2]{1,2,0:T(2,128)}, u32[]{:S(2)}) copy-start(s32[4,197,2]{1,2,0:T(2,128)} %param.29) | copy-start | bytes 18916
  133.9 50.9 %copy-start.33 = (s32[4,197,2]{1,2,0:T(2,128)S(1)}, s32[4,197,2]{1,2,0:T(2,128)}, u32[]{:S(2)}) copy-start(s32[4,197,2]{1,2,0:T(2,128)} %param.30) | copy-start | bytes 18916
  133.9 51.0 %copy-start.34 = (bf16[4,768]{1,0:T(4,128)(2,1)S(1)}, bf16[4,768]{1,0:T(4,128)(2,1)}, u32[]{:S(2)}) copy-start(bf16[4,768]{1,0:T(4,128)(2,1)} %param.26) | copy-start | bytes 18436
  133.9 56.9 %all-gather.17.cloned.1.call-start = ((), (), s32[]{:S(2)}) async-start(), calls=%async_computation.14 | async-start | bytes 1536000 | tf_op jit(solution)/shard_map/all_gather | solution.py:131
  134.7 63.2 %all-gather.11.cloned.1.call-start = ((), (), s32[]{:S(2)}) async-start(), calls=%async_computation.10 | async-start | bytes 1536000 | tf_op jit(solution)/shard_map/all_gather | solution.py:130
  161.0 23.8 %copy-start.31 = (f32[197]{0:T(256)}, f32[197]{0:T(256)S(1)}, u32[]{:S(2)}) copy-start(f32[197]{0:T(256)S(1)} %multiply_reduce_fusion.4) | copy-start | bytes 2368
  161.1 23.8 %copy-start.27 = (f32[197]{0:T(256)}, f32[197]{0:T(256)S(1)}, u32[]{:S(2)}) copy-start(f32[197]{0:T(256)S(1)} %fusion.83) | copy-start | bytes 2368
  163.0 117.2 %all-gather.13.cloned.1.call-start = ((), (), s32[]{:S(2)}) async-start(), calls=%async_computation.11 | async-start | bytes 5308416 | tf_op jit(solution)/shard_map/all_gather | solution.py:81
  163.6 196.9 %all-gather.15.cloned.1.call-start = ((), (), s32[]{:S(2)}) async-start(), calls=%async_computation.12 | async-start | bytes 5308416 | tf_op jit(solution)/shard_map/all_gather | solution.py:82
  164.1 257.2 %reduce-scatter.15.cloned.1.call-start = ((), (), s32[]{:S(2)}) async-start(), calls=%async_computation.15 | async-start | bytes 1536000 | tf_op jit(solution)/shard_map/reduce_scatter | solution.py:59
  184.9 193.0 %copy-start.24 = (f32[4,768]{1,0:T(4,128)}, f32[4,768]{1,0:T(4,128)S(1)}, u32[]{:S(2)}) copy-start(f32[4,768]{1,0:T(4,128)S(1)} %convert_element_type.194) | copy-start | bytes 36868
  386.8 21.4 %copy-start.40 = (u32[32]{0:T(128)S(1)}, u32[32]{0:T(128)}, u32[]{:S(2)}) copy-start(u32[32]{0:T(128)} %constant.98) | copy-start | bytes 388
  390.3 50.5 %all-gather.19.cloned.1.call-start = ((), (), s32[]{:S(2)}) async-start(), calls=%async_computation.16 | async-start | bytes 1536000 | tf_op jit(solution)/shard_map/all_gather | solution.py:234
  410.2 13.0 %copy-start.32 = (f32[197]{0:T(256)S(1)}, f32[197]{0:T(256)}, u32[]{:S(2)}) copy-start(f32[197]{0:T(256)} %copy-done.31) | copy-start | bytes 2368
  410.2 13.0 %copy-start.28 = (f32[197]{0:T(256)S(1)}, f32[197]{0:T(256)}, u32[]{:S(2)}) copy-start(f32[197]{0:T(256)} %copy-done.27) | copy-start | bytes 2368
  425.2 51.6 %reduce-scatter.17.cloned.1.call-start = ((), (), s32[]{:S(2)}) async-start(), calls=%async_computation.17 | async-start | bytes 1536000 | tf_op jit(solution)/shard_map/reduce_scatter | solution.py:59
  450.5 54.9 %reduce-scatter.13.cloned.1.call-start = ((), (), s32[]{:S(2)}) async-start(), calls=%async_computation.13 | async-start | bytes 1536000 | tf_op jit(solution)/shard_map/reduce_scatter | solution.py:59
  457.3 112.8 %reduce-scatter.25.cloned.1.call-start = ((), (), s32[]{:S(2)}) async-start(), calls=%async_computation.21 | async-start | bytes 442368
  460.3 176.6 %reduce-scatter.19.cloned.1.call-start = ((), (), s32[]{:S(2)}) async-start(), calls=%async_computation.18 | async-start | bytes 1327104 | tf_op jit(solution)/shard_map/reduce_scatter | solution.py:271
  464.2 13.8 %copy-start.30 = (f32[197]{0:T(256)S(1)}, f32[197]{0:T(256)}, u32[]{:S(2)}) copy-start(f32[197]{0:T(256)} %copy-done.29) | copy-start | bytes 2368
  464.2 15.3 %copy-start.6 = (f32[1,197,768]{2,1,0:T(8,128)S(1)}, f32[1,197,768]{2,1,0:T(8,128)}, u32[]{:S(2)}) copy-start(f32[1,197,768]{2,1,0:T(8,128)} %copy-done.5) | copy-start | bytes 1815556
  464.2 245.0 %all-reduce.10.cloned.1.call-start = ((), (), s32[]{:S(2)}) async-start(), calls=%async_computation.22 | async-start | bytes 180224
  464.9 16.9 %copy-start.25 = (f32[4,768]{1,0:T(4,128)S(1)}, f32[4,768]{1,0:T(4,128)}, u32[]{:S(2)}) copy-start(f32[4,768]{1,0:T(4,128)} %copy-done.24) | copy-start | bytes 36868
  481.8 325.4 %reduce-scatter.23.cloned.1.call-start = ((), (), s32[]{:S(2)}) async-start(), calls=%async_computation.20 | async-start | bytes 5308416 | tf_op jit(solution)/shard_map/reduce_scatter | solution.py:186
  490.3 415.9 %reduce-scatter.21.cloned.1.call-start = ((), (), s32[]{:S(2)}) async-start(), calls=%async_computation.19 | async-start | bytes 5308416 | tf_op jit(solution)/shard_map/reduce_scatter | solution.py:196
  (29 other events, 118.9 us)
Sparse Core Ops, SparseCore 0:
  56.6 14.9 all-gather.8
  134.1 24.5 reduce-scatter.10
  160.3 17.7 all-gather.16
  180.2 17.7 all-gather.10
  200.2 79.8 all-gather.12
  282.4 78.0 all-gather.14
  390.4 24.1 reduce-scatter.14
  425.3 15.4 all-gather.18
  450.7 26.0 reduce-scatter.16
  479.4 26.0 reduce-scatter.12
  508.7 61.2 reduce-scatter.24
  573.9 62.9 reduce-scatter.18
  640.8 68.3 all-reduce.9
  712.7 94.3 reduce-scatter.22
  810.6 95.5 reduce-scatter.20

commit v2 on v1

--- a/solution.py
+++ b/solution.py
@@ -1,6 +1,10 @@
+import functools
+
 import jax
 import jax.numpy as jnp
 from jax import lax
+from jax.experimental import pallas as pl
+from jax.experimental.pallas import tpu as pltpu
 from jax.sharding import PartitionSpec as P
 
 HEAD_DIM = 64
@@ -9,6 +13,275 @@
 
 EPSILON = 1e-06
 PRECISE = lax.Precision.HIGHEST
+
+
+MESH = pl.DeviceIdType.MESH
+LINE = 4
+SIDE = 2
+
+
+def greet(z, y, tensor):
+    barrier = pltpu.get_barrier_semaphore()
+    pl.semaphore_signal(
+        barrier, inc=1, device_id=(z * SIDE + 1 - y, tensor), device_id_type=MESH
+    )
+
+    @pl.when(z > 0)
+    def _():
+        pl.semaphore_signal(
+            barrier, inc=1, device_id=((z - 1) * SIDE + y, tensor), device_id_type=MESH
+        )
+
+    @pl.when(z < LINE - 1)
+    def _():
+        pl.semaphore_signal(
+            barrier, inc=1, device_id=((z + 1) * SIDE + y, tensor), device_id_type=MESH
+        )
+
+    @pl.when((z == 0) | (z == LINE - 1))
+    def _():
+        pl.semaphore_wait(barrier, 2)
+
+    @pl.when((z > 0) & (z < LINE - 1))
+    def _():
+        pl.semaphore_wait(barrier, 3)
+
+
+def gather_kernel(count, *refs):
+    sources = refs[:count]
+    outs = refs[count : 2 * count]
+    own_sem, side_send, up_send, down_send, arrived = refs[2 * count :]
+    place = lax.axis_index("dp")
+    tensor = lax.axis_index("tensor")
+    z = place // SIDE
+    y = place % SIDE
+    greet(z, y, tensor)
+
+    def send(piece, block, level, column, send_sem, first):
+        where = outs[piece].at[:, block]
+        return pltpu.make_async_remote_copy(
+            src_ref=sources[piece] if first else where,
+            dst_ref=where,
+            send_sem=send_sem,
+            recv_sem=arrived.at[piece, block],
+            device_id=(level * SIDE + column, tensor),
+            device_id_type=MESH,
+        )
+
+    def to_side(piece, level, first=False):
+        return send(
+            piece, level * SIDE + y, z, 1 - y, side_send.at[piece, level], first
+        )
+
+    def to_up(piece, level, first=False):
+        return send(piece, level * SIDE + y, z + 1, y, up_send.at[piece, level], first)
+
+    def to_down(piece, level, first=False):
+        return send(piece, level * SIDE + y, z - 1, y, down_send.at[piece, level], first)
+
+    for piece in range(count):
+
+        @pl.when(z < LINE - 1)
+        def _():
+            to_up(piece, z, True).start()
+
+        @pl.when(z > 0)
+        def _():
+            to_down(piece, z, True).start()
+
+        to_side(piece, z, True).start()
+        pltpu.make_async_copy(
+            sources[piece], outs[piece].at[:, place], own_sem.at[piece]
+        ).start()
+    for step in range(1, LINE):
+        for piece in range(count):
+
+            @pl.when(z - step >= 0)
+            def _():
+                came = to_down(piece, z - step)
+                came.wait_recv()
+
+                @pl.when(z < LINE - 1)
+                def _():
+                    to_up(piece, z - step).start()
+
+                to_side(piece, z - step).start()
+
+            @pl.when(z + step <= LINE - 1)
+            def _():
+                came = to_up(piece, z + step)
+                came.wait_recv()
+
+                @pl.when(z > 0)
+                def _():
+                    to_down(piece, z + step).start()
+
+                to_side(piece, z + step).start()
+
+    for piece in range(count):
+        pltpu.make_async_copy(
+            sources[piece], outs[piece].at[:, place], own_sem.at[piece]
+        ).wait()
+        for level in range(LINE):
+            send(
+                piece, level * SIDE + 1 - y, z, 1 - y, side_send.at[piece, level], False
+            ).wait_recv()
+            to_side(piece, level).wait_send()
+
+            @pl.when((z < LINE - 1) & (level <= z))
+            def _():
+                to_up(piece, level).wait_send()
+
+            @pl.when((z > 0) & (level >= z))
+            def _():
+                to_down(piece, level).wait_send()
+
+
+def gather_weights(*shards):
+    count = len(shards)
+    return pl.pallas_call(
+        functools.partial(gather_kernel, count),
+        out_shape=[
+            jax.ShapeDtypeStruct(
+                (shard.shape[0], LINE * SIDE) + shard.shape[1:], shard.dtype
+            )
+            for shard in shards
+        ],
+        in_specs=[pl.BlockSpec(memory_space=pl.ANY)] * count,
+        out_specs=[pl.BlockSpec(memory_space=pl.ANY)] * count,
+        scratch_shapes=[
+            pltpu.SemaphoreType.DMA((count,)),
+            pltpu.SemaphoreType.DMA((count, LINE)),
+            pltpu.SemaphoreType.DMA((count, LINE)),
+            pltpu.SemaphoreType.DMA((count, LINE)),
+            pltpu.SemaphoreType.DMA((count, LINE * SIDE)),
+        ],
+        compiler_params=pltpu.CompilerParams(collective_id=0, has_side_effects=True),
+    )(*shards)
+
+
+def reduce_kernel(count, *refs):
+    terms = refs[:count]
+    outs = refs[count : 2 * count]
+    side_in = refs[2 * count : 3 * count]
+    line_in = refs[3 * count : 4 * count]
+    passing = refs[4 * count : 5 * count]
+    side_send, side_recv, line_send, line_recv = refs[5 * count :]
+    place = lax.axis_index("dp")
+    tensor = lax.axis_index("tensor")
+    z = place // SIDE
+    y = place % SIDE
+    greet(z, y, tensor)
+    high = z // 2
+    depth = z + high * (3 - 2 * z)
+    inward = 1 - 2 * high
+    end = depth == 0
+    middle = depth == 1
+
+    def target(step):
+        mirrored = (3, 2, 1 - depth, depth)[step]
+        return mirrored + high * (3 - 2 * mirrored)
+
+    def to_side(piece, step):
+        return pltpu.make_async_remote_copy(
+            src_ref=terms[piece].at[:, target(step) * SIDE + 1 - y],
+            dst_ref=side_in[piece].at[step],
+            send_sem=side_send.at[piece, step],
+            recv_sem=side_recv.at[piece, step],
+            device_id=(z * SIDE + 1 - y, tensor),
+            device_id_type=MESH,
+        )
+
+    def to_line(piece, step, slot, move):
+        return pltpu.make_async_remote_copy(
+            src_ref=passing[piece].at[step],
+            dst_ref=line_in[piece].at[slot],
+            send_sem=line_send.at[piece, step],
+            recv_sem=line_recv.at[piece, slot],
+            device_id=((z + move) * SIDE + y, tensor),
+            device_id_type=MESH,
+        )
+
+    def add(piece, step, slots, dst):
+        slabs, _, rows, _ = terms[piece].shape
+        mine = terms[piece].at[:, target(step) * SIDE + y]
+        per = rows // 16
+
+        @pl.loop(0, slabs * per)
+        def _(at):
+            slab = at // per
+            part = pl.ds(pl.multiple_of((at % per) * 16, 16), 16)
+            total = mine[slab, part, :].astype(jnp.float32)
+            total += side_in[piece][step, slab, part, :].astype(jnp.float32)
+            for slot in slots:
+                total += line_in[piece][slot, slab, part, :].astype(jnp.float32)
+            dst[slab, part, :] = total.astype(dst.dtype)
+
+    for step in range(4):
+        for piece in range(count):
+            to_side(piece, step).start()
+
+    for step in range(4):
+        for piece in range(count):
+            to_side(piece, step).wait_recv()
+            if step < 3:
+
+                @pl.when(end)
+                def _():
+                    add(piece, step, (), passing[piece].at[step])
+                    to_line(piece, step, step, inward).start()
+
+                @pl.when(middle)
+                def _():
+                    slot = (0, 1, 3)[step]
+                    to_line(piece, step, slot, inward).wait_recv()
+                    add(piece, step, (slot,), passing[piece].at[step])
+                    if step < 2:
+                        to_line(piece, step, 3 + step, inward).start()
+                    else:
+                        to_line(piece, step, 4, -inward).start()
+
+            else:
+
+                @pl.when(end)
+                def _():
+                    to_line(piece, 0, 4, inward).wait_recv()
+                    add(piece, step, (4,), outs[piece])
+
+                @pl.when(middle)
+                def _():
+                    to_line(piece, 0, 2, inward).wait_recv()
+                    to_line(piece, 0, 4, inward).wait_recv()
+                    add(piece, step, (2, 4), outs[piece])
+
+    for piece in range(count):
+        for step in range(4):
+            to_side(piece, step).wait_send()
+        for step in range(3):
+            to_line(piece, step, step, inward).wait_send()
+
+
+def reduce_grads(*terms):
+    count = len(terms)
+    shards = [(term.shape[0],) + term.shape[2:] for term in terms]
+    return pl.pallas_call(
+        functools.partial(reduce_kernel, count),
+        out_shape=[jax.ShapeDtypeStruct(shard, jnp.float32) for shard in shards],
+        in_specs=[pl.BlockSpec(memory_space=pltpu.VMEM)] * count,
+        out_specs=[pl.BlockSpec(memory_space=pltpu.VMEM)] * count,
+        scratch_shapes=[pltpu.VMEM((4,) + shard, jnp.bfloat16) for shard in shards]
+        + [pltpu.VMEM((5,) + shard, jnp.bfloat16) for shard in shards]
+        + [pltpu.VMEM((3,) + shard, jnp.bfloat16) for shard in shards]
+        + [
+            pltpu.SemaphoreType.DMA((count, 4)),
+            pltpu.SemaphoreType.DMA((count, 4)),
+            pltpu.SemaphoreType.DMA((count, 3)),
+            pltpu.SemaphoreType.DMA((count, 5)),
+        ],
+        compiler_params=pltpu.CompilerParams(
+            collective_id=1, has_side_effects=True, vmem_limit_bytes=52 * 2**20
+        ),
+    )(*terms)
 
 
 def layer_norm(values, gain, bias):
@@ -67,24 +340,44 @@
         third = (rest - second.astype(jnp.float32)).astype(jnp.bfloat16)
         return jnp.concatenate([first, second, third], axis=-1)
 
-    def fetch_attention():
-        return (
-            lax.all_gather(qkv_weight, "dp", axis=0, tiled=True),
-            lax.all_gather(proj_weight, "dp", axis=1, tiled=True),
-            lax.all_gather(ln1_gain, "dp", axis=0, tiled=True),
-            lax.all_gather(ln1_bias, "dp", axis=0, tiled=True),
-            lax.all_gather(proj_bias, "dp", axis=0, tiled=True),
-        )
-
-    def fetch_experts():
-        return (
-            lax.all_gather(expert_in, "dp", axis=1, tiled=True),
-            lax.all_gather(expert_out, "dp", axis=2, tiled=True),
-            lax.all_gather(router_weight, "dp", axis=0, tiled=True),
-            lax.all_gather(expert_out_bias, "dp", axis=1, tiled=True),
-            lax.all_gather(ln2_gain, "dp", axis=0, tiled=True),
-            lax.all_gather(ln2_bias, "dp", axis=0, tiled=True),
-        )
+    share = model_width // dp_count
+    by_kernel = dp_count == LINE * SIDE and tensor_count == 4
+
+    def over_dp(shard):
+        return lax.all_gather(shard, "dp", axis=1)
+
+    attn_shard = jnp.concatenate(
+        [qkv_weight.reshape(share, -1), proj_weight.T], axis=1
+    )[None]
+    small_shard = jnp.concatenate(
+        [
+            jnp.stack([ln1_gain, ln1_bias, proj_bias, ln2_gain, ln2_bias], axis=1),
+            router_weight,
+            expert_out_bias.T,
+        ],
+        axis=1,
+    )
+    small_shard = jnp.pad(small_shard, ((0, 0), (0, 128 - small_shard.shape[1])))[None]
+    shards = (
+        small_shard,
+        attn_shard,
+        expert_in,
+        jnp.swapaxes(expert_out, 1, 2),
+    )
+    if by_kernel:
+        fetched = gather_weights(*shards)
+    else:
+        fetched = [over_dp(shard) for shard in shards]
+    small_full = fetched[0].reshape(model_width, 128)
+    attn_full = fetched[1].reshape(model_width, -1)
+    in_full = fetched[2].reshape(experts, model_width, -1)
+    out_full = fetched[3].reshape(experts, model_width, -1)
+    qkv_cols = 3 * heads_local * HEAD_DIM
+    qkv_full = attn_full[:, :qkv_cols].reshape(model_width, 3, -1)
+    proj_full = attn_full[:, qkv_cols:]
+    gain_one, bias_one, proj_shift, gain_two, bias_two = (small_full[:, k] for k in range(5))
+    router_full = small_full[:, 5 : 5 + experts]
+    back_shift = small_full[:, 5 + experts : 5 + 2 * experts].T
 
     def scores_of(query_heads, key_heads):
         return (
@@ -94,7 +387,6 @@
             * score_scale
         )
 
-    qkv_full, proj_full, gain_one, bias_one, proj_shift = fetch_attention()
     gain_one_f = gain_one.astype(jnp.float32)
     bias_one_f = bias_one.astype(jnp.float32)
     source = inputs.astype(jnp.float32)
@@ -120,10 +412,9 @@
         preferred_element_type=jnp.float32,
     )
     attended = attended.astype(jnp.bfloat16).reshape(group_images, seq_len, heads_local * HEAD_DIM)
-    attn_terms = jnp.einsum("bsf,fd->bsd", attended, proj_full, preferred_element_type=jnp.float32)
+    attn_terms = jnp.einsum("bsf,df->bsd", attended, proj_full, preferred_element_type=jnp.float32)
     attn_sum = scatter_rows(attn_terms)
     state = source + attn_sum + proj_shift.astype(jnp.float32)
-    in_full, out_full, router_full, back_shift, gain_two, bias_two = fetch_experts()
     gain_two_f = gain_two.astype(jnp.float32)
     bias_two_f = bias_two.astype(jnp.float32)
     normed_two = layer_norm(state, gain_two_f, bias_two_f).astype(jnp.bfloat16)
@@ -165,7 +456,7 @@
     )
     hidden = gelu_tanh(pre).astype(jnp.bfloat16)
     expert_terms = jnp.einsum(
-        "ecf,efd->ecd", hidden, out_full, preferred_element_type=jnp.float32
+        "ecf,edf->ecd", hidden, out_full, preferred_element_type=jnp.float32
     ).reshape(experts * slot_rows, model_width)
     gated_terms = (slot_gates[:, None] * expert_terms).astype(jnp.bfloat16)
     slot_dgate = jnp.sum(expert_terms * slot_out, axis=-1)
@@ -182,20 +473,14 @@
     result = state + mixed_sum + shift_own
     block_out = result.astype(jnp.bfloat16)
     own_grad = cotangent.astype(jnp.float32)
-    out_grad = jnp.einsum("ecf,ecd->efd", hidden, slot_grad, preferred_element_type=jnp.float32)
-    out_part = lax.psum_scatter(
-        out_grad.astype(jnp.bfloat16), "dp", scatter_dimension=2, tiled=True
-    ).astype(jnp.float32)
+    out_grad = jnp.einsum("ecf,ecd->edf", hidden, slot_grad, preferred_element_type=jnp.float32)
     hidden_grad = jnp.einsum(
-        "ecd,efd->ecf", slot_grad, out_full, preferred_element_type=jnp.float32
+        "ecd,edf->ecf", slot_grad, out_full, preferred_element_type=jnp.float32
     )
     gelu_pull = jax.vjp(gelu_tanh, pre)[1]
     pre_grad = gelu_pull(hidden_grad)[0].astype(jnp.bfloat16)
     in_grad = jnp.einsum("ecd,ecf->edf", dispatched, pre_grad, preferred_element_type=jnp.float32)
     in_bias_grad = jnp.sum(pre_grad.astype(jnp.float32), axis=1)
-    in_part = lax.psum_scatter(
-        in_grad.astype(jnp.bfloat16), "dp", scatter_dimension=1, tiled=True
-    ).astype(jnp.float32)
     slot_back = (
         jnp.einsum("ecf,edf->ecd", pre_grad, in_full, preferred_element_type=jnp.float32)
         .astype(jnp.bfloat16)
@@ -232,9 +517,9 @@
     state_grad = state_grad + own_grad
     proj_bias_grad = jnp.sum(state_grad, axis=(0, 1))
     state_rows = lax.all_gather(state_grad.astype(jnp.bfloat16), "tensor", axis=0, tiled=True)
-    proj_grad = jnp.einsum("bsf,bsd->fd", attended, state_rows, preferred_element_type=jnp.float32)
+    proj_grad = jnp.einsum("bsf,bsd->df", attended, state_rows, preferred_element_type=jnp.float32)
     attended_grad = jnp.einsum(
-        "bsd,fd->bsf", state_rows, proj_full, preferred_element_type=jnp.float32
+        "bsd,df->bsf", state_rows, proj_full, preferred_element_type=jnp.float32
     )
     attended_grad = attended_grad.astype(jnp.bfloat16).reshape(
         group_images, seq_len, heads_local, HEAD_DIM
@@ -268,60 +553,66 @@
     norm_one_pull = jax.vjp(layer_norm, source, gain_one_f, bias_one_f)[1]
     source_grad, gain_one_grad, bias_one_grad = norm_one_pull(normed_one_grad)
     input_grad = state_grad + source_grad
-    qkv_part = lax.psum_scatter(
-        qkv_grad.astype(jnp.bfloat16), "dp", scatter_dimension=0, tiled=True
-    ).astype(jnp.float32)
-    proj_part = lax.psum_scatter(
-        proj_grad.astype(jnp.bfloat16), "dp", scatter_dimension=1, tiled=True
-    ).astype(jnp.float32)
-    share = model_width // dp_count
     hidden_cols = in_bias_grad.shape[1]
     bias_share = hidden_cols // dp_count
-    bias_full = lax.dynamic_update_slice_in_dim(
-        jnp.zeros((experts, hidden_cols * tensor_count), jnp.float32),
-        in_bias_grad,
-        tensor_rank * hidden_cols,
-        1,
-    )
-    packed = jnp.concatenate(
+    attn_grad = jnp.concatenate(
+        [qkv_grad.reshape(model_width, qkv_cols), proj_grad], axis=1
+    )
+    small_grad = jnp.concatenate(
         [
-            gain_one_grad.reshape(dp_count, share),
-            bias_one_grad.reshape(dp_count, share),
-            proj_bias_grad.reshape(dp_count, share),
-            gain_two_grad.reshape(dp_count, share),
-            bias_two_grad.reshape(dp_count, share),
-            router_grad.reshape(dp_count, share * experts),
-            back_bias_grad.reshape(experts, dp_count, share).transpose(1, 0, 2).reshape(dp_count, -1),
-            bias_full.reshape(experts, dp_count, -1).transpose(1, 0, 2).reshape(dp_count, -1),
+            jnp.stack(
+                [gain_one_grad, bias_one_grad, proj_bias_grad, gain_two_grad, bias_two_grad],
+                axis=1,
+            ),
+            router_grad,
+            back_bias_grad.T,
+            in_bias_grad.T,
         ],
         axis=1,
     )
-    totals = lax.psum(
-        lax.psum_scatter(packed, "dp", scatter_dimension=0, tiled=True).reshape(-1), "tensor"
-    )
-    cuts = []
-    at = 0
-    for width in (share,) * 5 + (share * experts,) * 2:
-        cuts.append(totals[at : at + width])
-        at += width
-    in_bias_out = lax.dynamic_slice_in_dim(
-        totals[at:].reshape(experts, tensor_count * bias_share), tensor_rank * bias_share, bias_share, 1
-    )
+    small_grad = jnp.pad(small_grad, ((0, 0), (0, 128 - small_grad.shape[1])))
+
+    def blocks(values):
+        return values.astype(jnp.bfloat16).reshape(
+            -1, dp_count, values.shape[-2] // dp_count, values.shape[-1]
+        )
+
+    grads = [blocks(values) for values in (small_grad, attn_grad, in_grad, out_grad)]
+    if by_kernel:
+        small_part, attn_part, in_part, out_part = reduce_grads(*grads)
+    else:
+        small_part, attn_part, in_part, out_part = (
+            lax.psum_scatter(values, "dp", scatter_dimension=1).astype(jnp.float32)
+            for values in grads
+        )
+    small_part = small_part[0]
+    norm_cols = 5 + 2 * experts
+    totals = lax.psum(small_part[:, :norm_cols], "tensor")
+    moves = []
+    for source_dp in range(dp_count):
+        for source_tensor in range(tensor_count):
+            moves.append(
+                (source_dp * tensor_count + source_tensor, source_tensor * dp_count + source_dp)
+            )
+    in_bias_out = lax.ppermute(
+        small_part[:, norm_cols : norm_cols + experts].T, ("dp", "tensor"), moves
+    )
+    attn_part = attn_part[0]
     return (
         block_out,
         input_grad,
-        cuts[0],
-        cuts[1],
-        qkv_part,
-        proj_part,
-        cuts[2],
-        cuts[3],
-        cuts[4],
-        cuts[5].reshape(share, experts),
+        totals[:, 0],
+        totals[:, 1],
+        attn_part[:, :qkv_cols].reshape(share, 3, -1),
+        attn_part[:, qkv_cols:].T,
+        totals[:, 2],
+        totals[:, 3],
+        totals[:, 4],
+        totals[:, 5 : 5 + experts],
         in_part,
         in_bias_out,
-        out_part,
-        cuts[6].reshape(experts, share),
+        jnp.swapaxes(out_part, 1, 2),
+        totals[:, 5 + experts : norm_cols].T,
     )
 
 

time: 924 us -> 547 us (0.59)
  waiting for transfers between devices: 586 us -> 106 us
  Pallas kernels: 0 us -> 247 us
  blocking collectives: 164 us -> 20.9 us
    pallas_call x0 -> x2, Pallas kernels: none -> 247 us  [the longest x1 126 us: reduce_grads(): pl.pallas_call(functools.partial(reduce_kernel, count), out_shape=[jax.Sh...]
    reduce_scatter x3 -> x0, waiting for transfers between devices: 246 us -> none  [the longest x1 96.9 us: per_device(): lax.psum_scatter(in_grad.astype(jnp.bfloat16), 'dp', scatter_dimension=1,...]
    all_gather x2 -> x0, waiting for transfers between devices: 145 us -> none  [the longest x1 72.8 us: fetch_experts(): lax.all_gather(expert_out, 'dp', axis=2, tiled=True)]
    unnamed x17 -> x8, waiting for transfers between devices: 134 us -> 0.8 us
    all_gather x4 -> x0, blocking collectives: 105 us -> none  [the longest x1 36.2 us: fetch_attention(): lax.all_gather(qkv_weight, 'dp', axis=0, tiled=True)]
    unnamed x2 -> x1, blocking collectives: 49 us -> 10.2 us
    all_gather x1, waiting for transfers between devices: 0.01 us -> 17.3 us  [per_device(): rows_one = lax.all_gather(normed_one, 'tensor', axis=0, tiled=True)]
    reduce_scatter x4, waiting for transfers between devices: 42.3 us -> 57.3 us  [scatter_rows(): lax.psum_scatter(values.astype(jnp.bfloat16), 'tensor', scatter_dimension...]
  transfers between devices with their start and end apart: 15 -> 9, of which waited for: 12 -> 8; matrix products, arithmetic and copies ran while one was open for 9% -> 13% of each run, Pallas kernels for 0% -> 0%
where the time goes in v2:
time: 547 us; the launch traced here: 536 us
  Pallas kernels  247 us (45%)
  waiting for transfers between devices  106 us (19%)
  matrix products  81.7 us (15%)
  local copies, waits for them, and re-layouts  36.5 us (7%)
  other arithmetic  26.6 us (5%)
  blocking collectives  20.9 us (4%)
  between operations  15.5 us (3%)
    pallas_call x1, Pallas kernels, reduce_grads(): pl.pallas_call(functools.partial(reduce_kernel, count), out_shape=[jax.Sh...  126 us
    pallas_call x1, Pallas kernels, gather_weights(): pl.pallas_call(functools.partial(gather_kernel, count), out_shape=[jax.Sh...  122 us
    reduce_scatter x4, waiting for transfers between devices, scatter_rows(): lax.psum_scatter(values.astype(jnp.bfloat16), 'tensor', scatter_dimension...  57.3 us
    all_gather x1, waiting for transfers between devices, per_device(): rows_one = lax.all_gather(normed_one, 'tensor', axis=0, tiled=True)  17.3 us
    all_gather x1, waiting for transfers between devices, per_device(): rows_two = lax.all_gather(normed_two, 'tensor', axis=0, tiled=True)  17.2 us
    unnamed x101, local copies, waits for them, and re-layouts  13.7 us
  transfers between devices with their start and end apart: 9, of which 8 were waited for; matrix products, arithmetic and copies ran while one was open for 13% of the time, Pallas kernels for 0%

profile of v2, /device:TPU:0, one launch (start us, length us, event | category | flops | bytes accessed | tf_op | source)
XLA Modules:
  0.0 536.2 jit_solution(17273781583378872317)
XLA Ops:
  13.1 121.9 %shard_map.263 = (bf16[1,8,96,128]{3,2,1,0:T(8,128)(2,1)}, bf16[1,8,96,768]{3,2,1,0:T(8,128)(2,1)}, bf16[4,8,96,768]{3,2,1,0:T(8,128)(2,1)}, bf16[4,8,96,768]{3,2,1,0:T(8,128)(2,1)}) custom-call(bf16[1,96,128]{2,1,0:T(8,128)(2,1)} %pad_bitcast_fusion.refs_0_, bf16[1,96,768]{2,1,0:T(8,128)(2,1)} %maximum_bitcast_fusion.refs_1_, bf16[4,96,768]{2,1,0:T(8,128)(2,1)} %refs_2_.1, ...), custom_call_target="tpu_custom_call" | custom-call | tf_op jit(solution)/shard_map/pallas_call | solution.py:142
  139.2 17.3 %all-gather.5.cloned.1.call-done = bf16[4,197,768]{2,1,0:T(8,128)(2,1)} async-done(((bf16[1,197,768]{2,1,0:T(8,128)(2,1)}), bf16[4,197,768]{2,1,0:T(8,128)(2,1)}) %all-gather.5.cloned.1.call-update) | async-done | bytes 1210384 | tf_op jit(solution)/shard_map/all_gather | solution.py:394
  156.5 2.4 convolution_convert_fusion.7
  162.7 2.8 convolution_convert_fusion.6
  166.8 24.9 %reduce-scatter.5.cloned.1.call-done = bf16[1,197,768]{2,1,0:T(8,128)(2,1)} async-done(((bf16[4,197,768]{2,1,0:T(8,128)(2,1)}), bf16[1,197,768]{2,1,0:T(8,128)(2,1)}) %reduce-scatter.5.cloned.1.call-update) | async-done | bytes 302608 | tf_op jit(solution)/shard_map/reduce_scatter | solution.py:332
  196.3 2.5 fusion.2
  198.8 3.2 or.18
  202.1 9.1 %all-gather.9.cloned.1.call-done = bf16[4,197,768]{2,1,0:T(8,128)(2,1)} async-done(((bf16[1,197,768]{2,1,0:T(8,128)(2,1)}), bf16[4,197,768]{2,1,0:T(8,128)(2,1)}) %all-gather.9.cloned.1.call-update) | async-done | bytes 1210384 | tf_op jit(solution)/shard_map/all_gather | solution.py:422
  211.2 2.7 reshape.511
  213.9 17.2 %all-gather.7.cloned.1.call-done = bf16[4,197,768]{2,1,0:T(8,128)(2,1)} async-done(((bf16[1,197,768]{2,1,0:T(8,128)(2,1)}), bf16[4,197,768]{2,1,0:T(8,128)(2,1)}) %all-gather.7.cloned.1.call-update) | async-done | bytes 1210384 | tf_op jit(solution)/shard_map/all_gather | solution.py:421
  231.0 2.7 reshape.505
  233.8 5.3 convolution_convert_fusion
  239.6 5.7 %fusion.116 = f32[4,416,768]{2,1,0:T(8,128)S(1)} fusion(bf16[4,416,768]{2,1,0:T(8,128)(2,1)S(1)} %bitcast.246, bf16[4,768,768]{2,1,0:T(8,128)(2,1)} %bitcast.237), kind=kOutput, calls=%fused_computation.195 | convolution fusion | flops 1962934272 | bytes 12386304 | tf_op jit(solution)/shard_map/ecd,edf->ecf/dot_general | solution.py:454
  245.4 2.6 fusion.107
  248.0 5.9 %fusion.10 = (f32[1664]{0:T(1024)S(1)}, f32[1664,768]{1,0:T(8,128)}) fusion(f32[4,416,768]{2,1,0:T(8,128)S(1)} %fusion.107, bf16[788,768]{1,0:T(8,128)(2,1)S(1)} %copy-done.24, s32[788]{0:T(1024)S(1)} %get-tuple-element.111, s32[788]{0:T(1024)S(1)} %get-tuple-element.110), kind=kOutput, calls=%fused_computation.17 | convolution fusion | flops 2020540288 | bytes 11446944 | tf_op jit(solution)/shard_map/dot_general | solution.py:446
  255.6 2.9 multiply_convert_fusion
  258.6 8.2 %fusion.108 = (bf16[4,768]{1,0:T(4,128)(2,1)S(1)}, bf16[4,416,768]{2,1,0:T(8,128)(2,1)S(1)}) fusion(f32[4,416,768]{2,1,0:T(8,128)S(1)} %bitcast.235, f32[4,768]{1,0:T(4,128)S(1)} %convert_element_type.229, bf16[4,416,768]{2,1,0:T(8,128)(2,1)S(1)} %bitcast.248, bf16[4,768,768]{2,1,0:T(8,128)(2,1)} %bitcast.282), kind=kOutput, calls=%fused_computation.189 | convolution fusion | flops 1991046144 | bytes 14960640 | tf_op jit(solution)/shard_map/ecd,edf->ecf/dot_general | solution.py:477
  269.1 3.5 convolution_convert_fusion.4
  274.8 10.2 %all-reduce.2 = f32[4,197,4]{1,2,0:T(4,128)S(1)} all-reduce(f32[4,197,4]{1,2,0:T(4,128)S(1)} %copy.193), channel_id=5, replica_groups=mesh['dp'=8,'tensor'=4] {'tensor'}, use_global_device_ids=true, to_apply=%region_15.16.clone | all-reduce | flops 3152 | bytes 25216
  287.0 11.8 %reduce-scatter.9.cloned.1.call-done = bf16[1,197,768]{2,1,0:T(8,128)(2,1)} async-done(((bf16[4,197,768]{2,1,0:T(8,128)(2,1)}), bf16[1,197,768]{2,1,0:T(8,128)(2,1)}) %reduce-scatter.9.cloned.1.call-update) | async-done | bytes 302608 | tf_op jit(solution)/shard_map/reduce_scatter | solution.py:332
  302.8 3.7 reshape.522
  309.0 3.2 multiply_convert_fusion.1
  312.2 3.5 convolution_convert_fusion.5
  316.0 4.7 all-gather.11.cloned.1.call-done
  330.1 7.7 %convolution_convert_fusion.2 = bf16[4,768,768]{2,1,0:T(8,128)(2,1)} fusion(bf16[4,416,768]{2,1,0:T(8,128)(2,1)} %bitcast.247, bf16[4,416,768]{2,1,0:T(8,128)(2,1)} %copy-done.35), kind=kOutput, calls=%fused_computation.23 | convolution fusion | flops 1965293568 | bytes 9830400 | tf_op jit(solution)/shard_map/ecd,ecf->edf/dot_general | solution.py:482
  337.8 7.9 %convolution_convert_fusion.1 = bf16[4,768,768]{2,1,0:T(8,128)(2,1)} fusion(bf16[4,416,768]{2,1,0:T(8,128)(2,1)S(1)} %bitcast.249, f32[4,416,768]{2,1,0:T(8,128)} %copy-done.7, f32[4,768]{1,0:T(4,128)S(1)} %convert_element_type.229), kind=kOutput, calls=%fused_computation.22 | convolution fusion | flops 1978073088 | bytes 12398592 | tf_op jit(solution)/shard_map/ecf,ecd->edf/dot_general | solution.py:476
  345.7 3.5 reduce-scatter.7.cloned.1.call-done
  349.3 2.3 fusion.41
  351.6 2.9 reshape.523
  361.1 17.0 %reduce-scatter.11.cloned.1.call-done = bf16[1,197,768]{2,1,0:T(8,128)(2,1)} async-done(((bf16[4,197,768]{2,1,0:T(8,128)(2,1)}), bf16[1,197,768]{2,1,0:T(8,128)(2,1)}) %reduce-scatter.11.cloned.1.call-update) | async-done | bytes 302608 | tf_op jit(solution)/shard_map/reduce_scatter | solution.py:332
  383.7 125.6 %shard_map.264 = (f32[1,96,128]{2,1,0:T(8,128)S(1)}, f32[1,96,768]{2,1,0:T(8,128)S(1)}, f32[4,96,768]{2,1,0:T(8,128)S(1)}, f32[4,96,768]{2,1,0:T(8,128)}) custom-call(bf16[1,8,96,128]{3,2,1,0:T(8,128)(2,1)S(1)} %bitcast.224, bf16[1,8,96,768]{3,2,1,0:T(8,128)(2,1)} %pad_maximum_fusion.1.refs_1_, bf16[4,8,96,768]{3,2,1,0:T(8,128)(2,1)} %bitcast.241, ...), custom_call_target="tpu_custom_call" | custom-call | tf_op jit(solution)/shard_map/pallas_call | solution.py:267
  509.3 10.7 %psum.7 = f32[96,13]{1,0:T(8,128)S(1)} all-reduce(f32[96,13]{1,0:T(8,128)S(1)} %bitcast.228), channel_id=1, replica_groups=mesh['dp'=8,'tensor'=4] {'tensor'}, use_global_device_ids=true, to_apply=%region_29.30 | all-reduce | flops 1248 | bytes 9984 | tf_op jit(solution)/shard_map/psum | solution.py:590
  (210 shorter events, 65.1 us)
Async XLA Ops:
  7.2 129.8 %copy-start = (bf16[1,197,768]{2,1,0:T(8,128)(2,1)S(1)}, bf16[1,197,768]{2,1,0:T(8,128)(2,1)}, u32[]{:S(2)}) copy-start(bf16[1,197,768]{2,1,0:T(8,128)(2,1)} %param.16) | copy-start | bytes 907780
  7.2 149.3 %all-gather.5.cloned.1.call-start = ((), (), s32[]{:S(2)}) async-start(), calls=%async_computation.4 | async-start | bytes 1536000 | tf_op jit(solution)/shard_map/all_gather | solution.py:394
  138.4 53.4 %reduce-scatter.5.cloned.1.call-start = ((), (), s32[]{:S(2)}) async-start(), calls=%async_computation.5 | async-start | bytes 1536000 | tf_op jit(solution)/shard_map/reduce_scatter | solution.py:332
  139.2 19.7 %copy-start.26 = (bf16[768,576]{0,1:T(8,128)(2,1)}, bf16[768,576]{0,1:T(8,128)(2,1)S(1)}, u32[]{:S(2)}) copy-start(bf16[768,576]{0,1:T(8,128)(2,1)S(1)} %copy.182) | copy-start | bytes 2654212
  165.6 30.5 %copy-start.31 = (s32[4,197,2]{1,2,0:T(2,128)S(1)}, s32[4,197,2]{1,2,0:T(2,128)}, u32[]{:S(2)}) copy-start(s32[4,197,2]{1,2,0:T(2,128)} %param.29) | copy-start | bytes 18916
  165.6 30.6 %copy-start.32 = (s32[4,197,2]{1,2,0:T(2,128)S(1)}, s32[4,197,2]{1,2,0:T(2,128)}, u32[]{:S(2)}) copy-start(s32[4,197,2]{1,2,0:T(2,128)} %param.30) | copy-start | bytes 18916
  165.6 45.6 %all-gather.9.cloned.1.call-start = ((), (), s32[]{:S(2)}) async-start(), calls=%async_computation.8 | async-start | bytes 1536000 | tf_op jit(solution)/shard_map/all_gather | solution.py:422
  166.3 64.7 %all-gather.7.cloned.1.call-start = ((), (), s32[]{:S(2)}) async-start(), calls=%async_computation.6 | async-start | bytes 1536000 | tf_op jit(solution)/shard_map/all_gather | solution.py:421
  194.1 7.9 %copy-start.33 = (bf16[4,768]{1,0:T(4,128)(2,1)S(1)}, bf16[4,768]{1,0:T(4,128)(2,1)}, u32[]{:S(2)}) copy-start(bf16[4,768]{1,0:T(4,128)(2,1)} %param.26) | copy-start | bytes 18436
  196.1 102.7 %reduce-scatter.9.cloned.1.call-start = ((), (), s32[]{:S(2)}) async-start(), calls=%async_computation.9 | async-start | bytes 1536000 | tf_op jit(solution)/shard_map/reduce_scatter | solution.py:332
  233.8 5.3 copy-start.1
  233.8 5.3 copy-start.10
  239.1 6.3 %copy-start.12 = (bf16[1664,768]{1,0:T(8,128)(2,1)}, bf16[1664,768]{1,0:T(8,128)(2,1)S(1)}, u32[]{:S(2)}) copy-start(bf16[1664,768]{1,0:T(8,128)(2,1)S(1)} %convolution_convert_fusion) | copy-start | bytes 7667716
  239.1 6.3 %slice-start.4 = ((s8[4718592]{0:T(1024)(128)(4,1)}), s8[4194304]{0:T(1024)(128)(4,1)S(1)}, s32[]{:S(2)}) async-start(s8[4718592]{0:T(1024)(128)(4,1)} %bitcast.283), calls=%async_computation.16 | async-start | bytes 8388608
  239.6 5.7 %slice-start.5 = ((s8[4718592]{0:T(1024)(128)(4,1)}), s8[524288]{0:T(1024)(128)(4,1)S(1)}, s32[]{:S(2)}) async-start(s8[4718592]{0:T(1024)(128)(4,1)} %bitcast.283), calls=%async_computation.17 | async-start | bytes 1048576
  248.0 6.0 %copy-start.8 = (f32[4,416,768]{2,1,0:T(8,128)}, f32[4,416,768]{2,1,0:T(8,128)S(1)}, u32[]{:S(2)}) copy-start(f32[4,416,768]{2,1,0:T(8,128)S(1)} %fusion.107) | copy-start | bytes 15335428
  254.1 4.4 slice-start
  255.6 11.3 %slice-start.2 = ((s8[4718592]{0:T(1024)(128)(4,1)}), s8[4194304]{0:T(1024)(128)(4,1)S(1)}, s32[]{:S(2)}) async-start(s8[4718592]{0:T(1024)(128)(4,1)} %bitcast.238), calls=%async_computation.14 | async-start | bytes 8388608
  258.5 8.3 %copy-start.13 = (bf16[1664,768]{1,0:T(8,128)(2,1)}, bf16[1664,768]{1,0:T(8,128)(2,1)S(1)}, u32[]{:S(2)}) copy-start(bf16[1664,768]{1,0:T(8,128)(2,1)S(1)} %multiply_convert_fusion) | copy-start | bytes 7667716
  258.6 8.3 %slice-start.3 = ((s8[4718592]{0:T(1024)(128)(4,1)}), s8[524288]{0:T(1024)(128)(4,1)S(1)}, s32[]{:S(2)}) async-start(s8[4718592]{0:T(1024)(128)(4,1)} %bitcast.238), calls=%async_computation.15 | async-start | bytes 1048576
  272.6 48.0 %all-gather.11.cloned.1.call-start = ((), (), s32[]{:S(2)}) async-start(), calls=%async_computation.10 | async-start | bytes 1536000 | tf_op jit(solution)/shard_map/all_gather | solution.py:519
  273.4 25.4 %copy-start.2 = (bf16[1,197,768]{2,1,0:T(8,128)(2,1)S(1)}, bf16[1,197,768]{2,1,0:T(8,128)(2,1)}, u32[]{:S(2)}) copy-start(bf16[1,197,768]{2,1,0:T(8,128)(2,1)} %reduce-scatter.5.cloned.1.call-done) | copy-start | bytes 907780
  302.7 46.5 %reduce-scatter.7.cloned.1.call-start = ((), (), s32[]{:S(2)}) async-start(), calls=%async_computation.7 | async-start | bytes 1536000 | tf_op jit(solution)/shard_map/reduce_scatter | solution.py:332
  315.7 62.4 %reduce-scatter.11.cloned.1.call-start = ((), (), s32[]{:S(2)}) async-start(), calls=%async_computation.11 | async-start | bytes 1536000 | tf_op jit(solution)/shard_map/reduce_scatter | solution.py:332
  330.1 7.7 %copy-start.14 = (bf16[1664,768]{1,0:T(8,128)(2,1)S(1)}, bf16[1664,768]{1,0:T(8,128)(2,1)}, u32[]{:S(2)}) copy-start(bf16[1664,768]{1,0:T(8,128)(2,1)} %copy-done.13) | copy-start | bytes 7667716
  337.8 13.8 %copy-start.9 = (bf16[4,197,768]{2,1,0:T(8,128)(2,1)S(1)}, bf16[4,197,768]{2,1,0:T(8,128)(2,1)}, u32[]{:S(2)}) copy-start(bf16[4,197,768]{2,1,0:T(8,128)(2,1)} %all-gather.11.cloned.1.call-done) | copy-start | bytes 3631108
  345.7 8.8 %copy-start.19 = (bf16[4,3,64,197]{3,2,1,0:T(8,128)(2,1)S(1)}, bf16[4,3,64,197]{3,2,1,0:T(8,128)(2,1)}, u32[]{:S(2)}) copy-start(bf16[4,3,64,197]{3,2,1,0:T(8,128)(2,1)} %copy-done.18) | copy-start | bytes 907780
  345.7 8.8 %copy-start.21 = (bf16[4,3,64,197]{3,2,1,0:T(8,128)(2,1)S(1)}, bf16[4,3,64,197]{3,2,1,0:T(8,128)(2,1)}, u32[]{:S(2)}) copy-start(bf16[4,3,64,197]{3,2,1,0:T(8,128)(2,1)} %copy-done.20) | copy-start | bytes 907780
  359.8 22.0 %copy-start.4 = (bf16[1,197,768]{2,1,0:T(8,128)(2,1)S(1)}, bf16[1,197,768]{2,1,0:T(8,128)(2,1)}, u32[]{:S(2)}) copy-start(bf16[1,197,768]{2,1,0:T(8,128)(2,1)} %param.31) | copy-start | bytes 907780
  359.8 22.0 %copy-start.6 = (f32[1,197,768]{2,1,0:T(8,128)S(1)}, f32[1,197,768]{2,1,0:T(8,128)}, u32[]{:S(2)}) copy-start(f32[1,197,768]{2,1,0:T(8,128)} %copy-done.5) | copy-start | bytes 1815556
  520.2 6.0 %collective-permute-start = (f32[4,96]{0,1:T(8,128)S(1)}, f32[4,96]{0,1:T(8,128)S(1)}, u32[]{:S(2)}, u32[]{:S(2)}) collective-permute-start(f32[4,96]{0,1:T(8,128)S(1)} %slice_bitcast_fusion.14), channel_id=1, source_target_pairs={{0,0},{1,8},{2,16},{3,24},{4,1},{5,9},{6,17},{7,25},{8,2},{9,10},{... | collective-permute-start | bytes 4616 | tf_op jit(solution)/shard_map/ppermute | solution.py:597
  523.2 4.7 copy-start.25
  (19 other events, 43.2 us)
Sparse Core Ops, SparseCore 0:
  138.5 17.9 all-gather.4
  165.7 26.0 reduce-scatter.4
  193.4 17.7 all-gather.8
  213.3 17.7 all-gather.6
  272.7 26.0 reduce-scatter.8
  302.8 17.7 all-gather.10
  323.2 26.0 reduce-scatter.6
  352.0 26.0 reduce-scatter.10

commit v3 on v2

--- a/solution.py
+++ b/solution.py
@@ -157,6 +157,9 @@
             pltpu.SemaphoreType.DMA((count, LINE * SIDE)),
         ],
         compiler_params=pltpu.CompilerParams(collective_id=0, has_side_effects=True),
+        cost_estimate=pl.CostEstimate(
+            flops=0, bytes_accessed=400_000_000, transcendentals=0
+        ),
     )(*shards)
 
 
@@ -329,9 +332,14 @@
         return lax.dynamic_slice_in_dim(values, tensor_rank * local_images, local_images, 0)
 
     def scatter_rows(values):
-        return lax.psum_scatter(
-            values.astype(jnp.bfloat16), "tensor", scatter_dimension=0, tiled=True
-        ).astype(jnp.float32)
+        low = values.astype(jnp.bfloat16)
+        total = own_rows(values)
+        for hop in range(1, tensor_count):
+            there = lax.rem(tensor_rank + hop, tensor_count)
+            part = lax.dynamic_slice_in_dim(low, there * local_images, local_images, 0)
+            ring = [(rank, (rank + hop) % tensor_count) for rank in range(tensor_count)]
+            total = total + lax.ppermute(part, "tensor", ring).astype(jnp.float32)
+        return total
 
     def split_three(values):
         first = values.astype(jnp.bfloat16)
@@ -341,6 +349,9 @@
         return jnp.concatenate([first, second, third], axis=-1)
 
     share = model_width // dp_count
+    both_rows = lax.all_gather(
+        jnp.stack([inputs, cotangent], axis=1), "tensor", axis=0, tiled=True
+    )
     by_kernel = dp_count == LINE * SIDE and tensor_count == 4
 
     def over_dp(shard):
@@ -390,8 +401,9 @@
     gain_one_f = gain_one.astype(jnp.float32)
     bias_one_f = bias_one.astype(jnp.float32)
     source = inputs.astype(jnp.float32)
-    normed_one = layer_norm(source, gain_one_f, bias_one_f).astype(jnp.bfloat16)
-    rows_one = lax.all_gather(normed_one, "tensor", axis=0, tiled=True)
+    rows_one = layer_norm(
+        both_rows[:, 0].astype(jnp.float32), gain_one_f, bias_one_f
+    ).astype(jnp.bfloat16)
     mixed = jnp.einsum(
         "bsd,dkf->bskf", rows_one, qkv_full, preferred_element_type=jnp.float32
     ).astype(jnp.bfloat16)
@@ -419,7 +431,7 @@
     bias_two_f = bias_two.astype(jnp.float32)
     normed_two = layer_norm(state, gain_two_f, bias_two_f).astype(jnp.bfloat16)
     rows_two = lax.all_gather(normed_two, "tensor", axis=0, tiled=True)
-    out_rows = lax.all_gather(cotangent, "tensor", axis=0, tiled=True)
+    out_rows = both_rows[:, 1]
     token_rows = rows_two.reshape(tokens, model_width)
     grad_rows = out_rows.reshape(tokens, model_width)
     choice_ids = expert_ids.reshape(tokens, 2)

time: 547 us -> 503 us (0.920)
  waiting for transfers between devices: 106 us -> 54.1 us
  local copies, waits for them, and re-layouts: 36.5 us -> 46.8 us
  starting transfers between devices: 1.2 us -> 7.92 us
    reduce_scatter x4 -> x0, waiting for transfers between devices: 57.3 us -> none  [scatter_rows(): lax.psum_scatter(values.astype(jnp.bfloat16), 'tensor', scatter_dimension...]
    ppermute x0 -> x12, waiting for transfers between devices: none -> 47.3 us  [scatter_rows(): total = total + lax.ppermute(part, 'tensor', ring).astype(jnp.float32)]
    all_gather x2 -> x1, waiting for transfers between devices: 26.4 us -> 0.02 us  [per_device(): lax.all_gather(jnp.stack([inputs, cotangent], axis=1), 'tensor', axis=0,...]
    slice x0 -> x1, local copies, waits for them, and re-layouts: none -> 11.8 us  [per_device(): out_rows = both_rows[:, 1]]
    all_gather x1, waiting for transfers between devices: 17.2 us -> 6.71 us  [per_device(): rows_two = lax.all_gather(normed_two, 'tensor', axis=0, tiled=True)]
    ppermute x0 -> x12, starting transfers between devices: none -> 5.55 us  [scatter_rows(): total = total + lax.ppermute(part, 'tensor', ring).astype(jnp.float32)]
    unnamed x101 -> x109, local copies, waits for them, and re-layouts: 13.7 us -> 12.6 us
  transfers between devices with their start and end apart: 9 -> 16, of which waited for: 8 -> 11; matrix products, arithmetic and copies ran while one was open for 13% -> 10% of each run, Pallas kernels for 0% -> 25%
where the time goes in v3:
time: 503 us; the launch traced here: 495 us
  Pallas kernels  247 us (49%)
  matrix products  79.4 us (16%)
  waiting for transfers between devices  54.1 us (11%)
  local copies, waits for them, and re-layouts  46.8 us (9%)
  other arithmetic  22.8 us (5%)
  blocking collectives  21.6 us (4%)
  between operations  15 us (3%)
  starting transfers between devices  7.92 us (2%)
    pallas_call x1, Pallas kernels, reduce_grads(): pl.pallas_call(functools.partial(reduce_kernel, count), out_shape=[jax.Sh...  125 us
    pallas_call x1, Pallas kernels, gather_weights(): pl.pallas_call(functools.partial(gather_kernel, count), out_shape=[jax.Sh...  122 us
    ppermute x12, waiting for transfers between devices, scatter_rows(): total = total + lax.ppermute(part, 'tensor', ring).astype(jnp.float32)  47.3 us
    unnamed x109, local copies, waits for them, and re-layouts  12.6 us
    slice x1, local copies, waits for them, and re-layouts, per_device(): out_rows = both_rows[:, 1]  11.8 us
    psum x1, blocking collectives, per_device(): totals = lax.psum(small_part[:, :norm_cols], 'tensor')  10.9 us
    unnamed x1, blocking collectives  10.7 us
  transfers between devices with their start and end apart: 16, of which 11 were waited for; matrix products, arithmetic and copies ran while one was open for 10% of the time, Pallas kernels for 25%

profile of v3, /device:TPU:0, one launch (start us, length us, event | category | flops | bytes accessed | tf_op | source)
XLA Modules:
  0.0 494.6 jit_solution(8291944918383282927)
XLA Ops:
  12.0 121.9 %shard_map.263 = (bf16[1,8,96,128]{3,2,1,0:T(8,128)(2,1)}, bf16[1,8,96,768]{3,2,1,0:T(8,128)(2,1)}, bf16[4,8,96,768]{3,2,1,0:T(8,128)(2,1)}, bf16[4,8,96,768]{3,2,1,0:T(8,128)(2,1)}) custom-call(bf16[1,96,128]{2,1,0:T(8,128)(2,1)} %pad_bitcast_fusion.refs_0_, bf16[1,96,768]{2,1,0:T(8,128)(2,1)} %maximum_bitcast_fusion.refs_1_, bf16[4,96,768]{2,1,0:T(8,128)(2,1)} %refs_2_.1, ...), custom_call_target="tpu_custom_call" | custom-call | bytes 400000000 | tf_op jit(solution)/shard_map/pallas_call | solution.py:142
  136.5 11.8 %slice_reduce_fusion = (bf16[4,197,768]{2,1,0:T(8,128)(2,1)}, bf16[4,1,197,768]{3,1,2,0:T(2,128)(2,1)S(1)}) fusion(bf16[4,2,197,768]{3,1,2,0:T(2,128)(2,1)} %all-gather.4.cloned.1.call-done), kind=kLoop, calls=%fused_computation.37 | loop fusion | bytes 4841472 | tf_op jit(solution)/shard_map/slice | solution.py:434
  154.7 3.4 fusion.125
  161.3 4.9 collective-permute-done.2
  166.1 9.3 %collective-permute-done.1 = bf16[1,197,768]{2,1,0:T(8,128)(2,1)S(1)} collective-permute-done((bf16[1,197,768]{2,1,0:T(8,128)(2,1)}, bf16[1,197,768]{2,1,0:T(8,128)(2,1)S(1)}, u32[]{:S(2)}, u32[]{:S(2)}) %collective-permute-start.1) | collective-permute-done | bytes 302624 | tf_op jit(solution)/shard_map/ppermute | solution.py:341
  182.7 2.7 reshape_squeeze.3
  185.9 2.7 reshape.527
  188.6 6.7 %all-gather.6.cloned.1.call-done = bf16[4,197,768]{2,1,0:T(8,128)(2,1)} async-done(((bf16[1,197,768]{2,1,0:T(8,128)(2,1)}), bf16[4,197,768]{2,1,0:T(8,128)(2,1)}) %all-gather.6.cloned.1.call-update) | async-done | bytes 1210384 | tf_op jit(solution)/shard_map/all_gather | solution.py:433
  196.9 4.6 convolution_convert_fusion
  202.1 5.3 %fusion.130 = f32[4,416,768]{2,1,0:T(8,128)S(1)} fusion(bf16[4,416,768]{2,1,0:T(8,128)(2,1)} %bitcast.259, bf16[4,768,768]{2,1,0:T(8,128)(2,1)} %bitcast.250), kind=kOutput, calls=%fused_computation.220 | convolution fusion | flops 1962934272 | bytes 12386304 | tf_op jit(solution)/shard_map/ecd,edf->ecf/dot_general | solution.py:466
  207.4 6.6 %fusion.114 = f32[4,416,768]{2,1,0:T(8,128)S(1)} fusion(bf16[4,768,768]{2,1,0:T(8,128)(2,1)} %bitcast.294, f32[4,416,768]{2,1,0:T(8,128)S(1)} %fusion.130, f32[4,768]{1,0:T(4,128)S(1)} %convert_element_type.268), kind=kOutput, calls=%fused_computation.207 | convolution fusion | flops 1975713792 | bytes 14954496 | tf_op jit(solution)/shard_map/ecf,edf->ecd/dot_general | solution.py:470
  214.1 5.9 %fusion.10 = (f32[1664]{0:T(1024)S(1)}, f32[1664,768]{1,0:T(8,128)}) fusion(f32[4,416,768]{2,1,0:T(8,128)S(1)} %fusion.114, bf16[788,768]{1,0:T(8,128)(2,1)S(1)} %copy-done.20, s32[788]{0:T(1024)S(1)} %get-tuple-element.114, s32[788]{0:T(1024)S(1)} %get-tuple-element.113), kind=kOutput, calls=%fused_computation.17 | convolution fusion | flops 2020540288 | bytes 11446944 | tf_op jit(solution)/shard_map/dot_general | solution.py:458
  222.2 2.8 multiply_convert_fusion.1
  226.4 10.7 %all-reduce.2 = f32[4,197,4]{1,2,0:T(4,128)S(1)} all-reduce(f32[4,197,4]{1,2,0:T(4,128)S(1)} %copy.197), channel_id=2, replica_groups=mesh['dp'=8,'tensor'=4] {'tensor'}, use_global_device_ids=true, to_apply=%region_12.13.clone | all-reduce | flops 3152 | bytes 25216
  237.1 2.9 multiply_convert_fusion
  240.1 8.8 %fusion.116 = (bf16[4,768]{1,0:T(4,128)(2,1)S(1)}, bf16[4,416,768]{2,1,0:T(8,128)(2,1)S(1)}) fusion(f32[4,416,768]{2,1,0:T(8,128)} %copy-done.9, f32[4,768]{1,0:T(4,128)S(1)} %copy-done.32, bf16[4,416,768]{2,1,0:T(8,128)(2,1)S(1)} %bitcast.261, bf16[4,768,768]{2,1,0:T(8,128)(2,1)} %bitcast.295), kind=kOutput, calls=%fused_computation.209 | convolution fusion | flops 1991046144 | bytes 14960640 | tf_op jit(solution)/shard_map/ecd,edf->ecf/dot_general | solution.py:489
  249.0 2.2 convolution_convert_fusion.3
  251.2 4.2 fusion.127
  255.5 2.4 fusion.128
  261.1 3.4 collective-permute-done.8
  264.5 9.8 %collective-permute-done.7 = bf16[1,197,768]{2,1,0:T(8,128)(2,1)S(1)} collective-permute-done((bf16[1,197,768]{2,1,0:T(8,128)(2,1)S(1)}, bf16[1,197,768]{2,1,0:T(8,128)(2,1)S(1)}, u32[]{:S(2)}, u32[]{:S(2)}) %collective-permute-start.7) | collective-permute-done | bytes 302624 | tf_op jit(solution)/shard_map/ppermute | solution.py:341
  277.3 7.5 %convolution_convert_fusion.2 = bf16[4,768,768]{2,1,0:T(8,128)(2,1)} fusion(bf16[4,416,768]{2,1,0:T(8,128)(2,1)} %bitcast.260, bf16[4,416,768]{2,1,0:T(8,128)(2,1)} %copy-done.43), kind=kOutput, calls=%fused_computation.26 | convolution fusion | flops 1965293568 | bytes 9830400 | tf_op jit(solution)/shard_map/ecd,ecf->edf/dot_general | solution.py:494
  285.6 7.6 %convolution_convert_fusion.1 = bf16[4,768,768]{2,1,0:T(8,128)(2,1)} fusion(bf16[4,416,768]{2,1,0:T(8,128)(2,1)S(1)} %bitcast.262, f32[4,416,768]{2,1,0:T(8,128)} %copy-done.9, f32[4,768]{1,0:T(4,128)S(1)} %copy-done.32), kind=kOutput, calls=%fused_computation.25 | convolution fusion | flops 1978073088 | bytes 12398592 | tf_op jit(solution)/shard_map/ecf,ecd->edf/dot_general | solution.py:488
  293.8 4.4 collective-permute-done.5
  298.2 8.1 %collective-permute-done.4 = bf16[1,197,768]{2,1,0:T(8,128)(2,1)S(1)} collective-permute-done((bf16[1,197,768]{2,1,0:T(8,128)(2,1)S(1)}, bf16[1,197,768]{2,1,0:T(8,128)(2,1)S(1)}, u32[]{:S(2)}, u32[]{:S(2)}) %collective-permute-start.4) | collective-permute-done | bytes 302624 | tf_op jit(solution)/shard_map/ppermute | solution.py:341
  306.7 2.4 add_convert_fusion
  314.7 2.7 fusion.129
  320.7 2.6 reshape.528
  323.3 3.1 fusion.33
  328.4 6.0 %collective-permute-done.10 = bf16[1,197,768]{2,1,0:T(8,128)(2,1)} collective-permute-done((bf16[1,197,768]{2,1,0:T(8,128)(2,1)}, bf16[1,197,768]{2,1,0:T(8,128)(2,1)}, u32[]{:S(2)}, u32[]{:S(2)}) %collective-permute-start.10) | collective-permute-done | bytes 302624 | tf_op jit(solution)/shard_map/ppermute | solution.py:341
  338.5 125.0 %shard_map.264 = (f32[1,96,128]{2,1,0:T(8,128)S(1)}, f32[1,96,768]{2,1,0:T(8,128)S(1)}, f32[4,96,768]{2,1,0:T(8,128)S(1)}, f32[4,96,768]{2,1,0:T(8,128)}) custom-call(bf16[1,8,96,128]{3,2,1,0:T(8,128)(2,1)S(1)} %bitcast.237, bf16[1,8,96,768]{3,2,1,0:T(8,128)(2,1)} %pad_maximum_fusion.1.refs_1_, bf16[4,8,96,768]{3,2,1,0:T(8,128)(2,1)} %bitcast.254, ...), custom_call_target="tpu_custom_call" | custom-call | tf_op jit(solution)/shard_map/pallas_call | solution.py:270
  464.2 10.9 %psum.7 = f32[96,13]{1,0:T(8,128)S(1)} all-reduce(f32[96,13]{1,0:T(8,128)S(1)} %bitcast.241), channel_id=1, replica_groups=mesh['dp'=8,'tensor'=4] {'tensor'}, use_global_device_ids=true, to_apply=%region_27.28 | all-reduce | flops 1248 | bytes 9984 | tf_op jit(solution)/shard_map/psum | solution.py:602
  (232 shorter events, 66.1 us)
Async XLA Ops:
  7.3 129.3 %all-gather.4.cloned.1.call-start = ((), (), s32[]{:S(2)}) async-start(), calls=%async_computation | async-start | bytes 3025920 | tf_op jit(solution)/shard_map/all_gather | solution.py:352
  9.8 185.4 %all-gather.6.cloned.1.call-start = ((), (), s32[]{:S(2)}) async-start(), calls=%async_computation.1 | async-start | bytes 1536000 | tf_op jit(solution)/shard_map/all_gather | solution.py:433
  135.9 13.3 %copy-start.22 = (bf16[768,576]{0,1:T(8,128)(2,1)}, bf16[768,576]{0,1:T(8,128)(2,1)S(1)}, u32[]{:S(2)}) copy-start(bf16[768,576]{0,1:T(8,128)(2,1)S(1)} %copy.186) | copy-start | bytes 2654212
  154.7 20.7 %copy-start.5 = (bf16[1,197,768]{2,1,0:T(8,128)(2,1)S(1)}, bf16[1,197,768]{2,1,0:T(8,128)(2,1)}, u32[]{:S(2)}) copy-start(bf16[1,197,768]{2,1,0:T(8,128)(2,1)} %param.16) | copy-start | bytes 907780
  159.1 7.1 %collective-permute-start.2 = (bf16[1,197,768]{2,1,0:T(8,128)(2,1)}, bf16[1,197,768]{2,1,0:T(8,128)(2,1)S(1)}, u32[]{:S(2)}, u32[]{:S(2)}) collective-permute-start(bf16[1,197,768]{2,1,0:T(8,128)(2,1)} %get-tuple-element.140), channel_id=1, source_target_pairs={{0,3},{1,0},{2,1},{3,2},{4,7},{5,4},{6,5},{7,6},{8,11},{9,8},{10,9... | collective-permute-start | bytes 907784 | tf_op jit(solution)/shard_map/ppermute | solution.py:341
  159.1 16.3 %collective-permute-start.1 = (bf16[1,197,768]{2,1,0:T(8,128)(2,1)}, bf16[1,197,768]{2,1,0:T(8,128)(2,1)S(1)}, u32[]{:S(2)}, u32[]{:S(2)}) collective-permute-start(bf16[1,197,768]{2,1,0:T(8,128)(2,1)} %get-tuple-element.141), channel_id=1, source_target_pairs={{0,2},{1,3},{2,0},{3,1},{4,6},{5,7},{6,4},{7,5},{8,10},{9,11},{10,... | collective-permute-start | bytes 907784 | tf_op jit(solution)/shard_map/ppermute | solution.py:341
  160.6 14.9 %collective-permute-start = (bf16[1,197,768]{2,1,0:T(8,128)(2,1)}, bf16[1,197,768]{2,1,0:T(8,128)(2,1)S(1)}, u32[]{:S(2)}, u32[]{:S(2)}) collective-permute-start(bf16[1,197,768]{2,1,0:T(8,128)(2,1)} %get-tuple-element.139), channel_id=1, source_target_pairs={{0,1},{1,2},{2,3},{3,0},{4,5},{5,6},{6,7},{7,4},{8,9},{9,10},{10,1... | collective-permute-start | bytes 907784 | tf_op jit(solution)/shard_map/ppermute | solution.py:341
  160.8 17.5 %copy-start.30 = (s32[4,197,2]{1,2,0:T(2,128)S(1)}, s32[4,197,2]{1,2,0:T(2,128)}, u32[]{:S(2)}) copy-start(s32[4,197,2]{1,2,0:T(2,128)} %param.29) | copy-start | bytes 18916
  160.8 17.5 %copy-start.33 = (s32[4,197,2]{1,2,0:T(2,128)S(1)}, s32[4,197,2]{1,2,0:T(2,128)}, u32[]{:S(2)}) copy-start(s32[4,197,2]{1,2,0:T(2,128)} %param.30) | copy-start | bytes 18916
  178.1 131.0 %all-gather.8.cloned.1.call-start = ((), (), s32[]{:S(2)}) async-start(), calls=%async_computation.2 | async-start | bytes 1536000 | tf_op jit(solution)/shard_map/all_gather | solution.py:531
  182.0 25.4 %copy-start.31 = (f32[4,768]{1,0:T(4,128)}, f32[4,768]{1,0:T(4,128)S(1)}, u32[]{:S(2)}) copy-start(f32[4,768]{1,0:T(4,128)S(1)} %convert_element_type.268) | copy-start | bytes 36868
  237.1 11.8 %slice-start = ((s8[4718592]{0:T(1024)(128)(4,1)}), s8[4194304]{0:T(1024)(128)(4,1)S(1)}, s32[]{:S(2)}) async-start(s8[4718592]{0:T(1024)(128)(4,1)} %bitcast.251), calls=%async_computation.3 | async-start | bytes 8388608
  240.1 8.9 %copy-start.13 = (bf16[1664,768]{1,0:T(8,128)(2,1)}, bf16[1664,768]{1,0:T(8,128)(2,1)S(1)}, u32[]{:S(2)}) copy-start(bf16[1664,768]{1,0:T(8,128)(2,1)S(1)} %multiply_convert_fusion) | copy-start | bytes 7667716
  240.1 8.9 %slice-start.1 = ((s8[4718592]{0:T(1024)(128)(4,1)}), s8[524288]{0:T(1024)(128)(4,1)S(1)}, s32[]{:S(2)}) async-start(s8[4718592]{0:T(1024)(128)(4,1)} %bitcast.251), calls=%async_computation.4 | async-start | bytes 1048576
  258.0 6.5 %collective-permute-start.8 = (bf16[1,197,768]{2,1,0:T(8,128)(2,1)S(1)}, bf16[1,197,768]{2,1,0:T(8,128)(2,1)S(1)}, u32[]{:S(2)}, u32[]{:S(2)}) collective-permute-start(bf16[1,197,768]{2,1,0:T(8,128)(2,1)S(1)} %get-tuple-element.134), channel_id=1, source_target_pairs={{0,3},{1,0},{2,1},{3,2},{4,7},{5,4},{6,5},{7,6},{8,11},{9,8},{10,9... | collective-permute-start | bytes 907784 | tf_op jit(solution)/shard_map/ppermute | solution.py:341
  258.1 16.3 %collective-permute-start.7 = (bf16[1,197,768]{2,1,0:T(8,128)(2,1)S(1)}, bf16[1,197,768]{2,1,0:T(8,128)(2,1)S(1)}, u32[]{:S(2)}, u32[]{:S(2)}) collective-permute-start(bf16[1,197,768]{2,1,0:T(8,128)(2,1)S(1)} %get-tuple-element.135), channel_id=1, source_target_pairs={{0,2},{1,3},{2,0},{3,1},{4,6},{5,7},{6,4},{7,5},{8,10},{9,11},{10,... | collective-permute-start | bytes 907784 | tf_op jit(solution)/shard_map/ppermute | solution.py:341
  259.8 14.6 %collective-permute-start.6 = (bf16[1,197,768]{2,1,0:T(8,128)(2,1)S(1)}, bf16[1,197,768]{2,1,0:T(8,128)(2,1)S(1)}, u32[]{:S(2)}, u32[]{:S(2)}) collective-permute-start(bf16[1,197,768]{2,1,0:T(8,128)(2,1)S(1)} %get-tuple-element.133), channel_id=1, source_target_pairs={{0,1},{1,2},{2,3},{3,0},{4,5},{5,6},{6,7},{7,4},{8,9},{9,10},{10,1... | collective-permute-start | bytes 907784 | tf_op jit(solution)/shard_map/ppermute | solution.py:341
  277.3 7.5 %copy-start.24 = (bf16[4,197,768]{2,1,0:T(8,128)(2,1)S(1)}, bf16[4,197,768]{2,1,0:T(8,128)(2,1)}, u32[]{:S(2)}) copy-start(bf16[4,197,768]{2,1,0:T(8,128)(2,1)} %get-tuple-element.166) | copy-start | bytes 3631108
  277.3 8.3 %copy-start.14 = (bf16[1664,768]{1,0:T(8,128)(2,1)S(1)}, bf16[1664,768]{1,0:T(8,128)(2,1)}, u32[]{:S(2)}) copy-start(bf16[1664,768]{1,0:T(8,128)(2,1)} %copy-done.13) | copy-start | bytes 7667716
  284.9 13.3 %collective-permute-start.5 = (bf16[1,197,768]{2,1,0:T(8,128)(2,1)S(1)}, bf16[1,197,768]{2,1,0:T(8,128)(2,1)S(1)}, u32[]{:S(2)}, u32[]{:S(2)}) collective-permute-start(bf16[1,197,768]{2,1,0:T(8,128)(2,1)S(1)} %get-tuple-element.137), channel_id=1, source_target_pairs={{0,3},{1,0},{2,1},{3,2},{4,7},{5,4},{6,5},{7,6},{8,11},{9,8},{10,9... | collective-permute-start | bytes 907784 | tf_op jit(solution)/shard_map/ppermute | solution.py:341
  285.0 21.4 %collective-permute-start.4 = (bf16[1,197,768]{2,1,0:T(8,128)(2,1)S(1)}, bf16[1,197,768]{2,1,0:T(8,128)(2,1)S(1)}, u32[]{:S(2)}, u32[]{:S(2)}) collective-permute-start(bf16[1,197,768]{2,1,0:T(8,128)(2,1)S(1)} %get-tuple-element.138), channel_id=1, source_target_pairs={{0,2},{1,3},{2,0},{3,1},{4,6},{5,7},{6,4},{7,5},{8,10},{9,11},{10,... | collective-permute-start | bytes 907784 | tf_op jit(solution)/shard_map/ppermute | solution.py:341
  285.5 8.0 %copy-start.12 = (bf16[1,197,768]{2,1,0:T(8,128)(2,1)S(1)}, bf16[1,197,768]{2,1,0:T(8,128)(2,1)}, u32[]{:S(2)}) copy-start(bf16[1,197,768]{2,1,0:T(8,128)(2,1)} %add_convert_fusion.1) | copy-start | bytes 907780
  285.5 21.2 %collective-permute-start.3 = (bf16[1,197,768]{2,1,0:T(8,128)(2,1)S(1)}, bf16[1,197,768]{2,1,0:T(8,128)(2,1)S(1)}, u32[]{:S(2)}, u32[]{:S(2)}) collective-permute-start(bf16[1,197,768]{2,1,0:T(8,128)(2,1)S(1)} %get-tuple-element.136), channel_id=1, source_target_pairs={{0,1},{1,2},{2,3},{3,0},{4,5},{5,6},{6,7},{7,4},{8,9},{9,10},{10,1... | collective-permute-start | bytes 907784 | tf_op jit(solution)/shard_map/ppermute | solution.py:341
  293.5 17.7 %copy-start.2 = (f32[4,3,197,197]{2,3,1,0:T(8,128)S(1)}, f32[4,3,197,197]{2,3,1,0:T(8,128)}, u32[]{:S(2)}) copy-start(f32[4,3,197,197]{2,3,1,0:T(8,128)} %copy-done.1) | copy-start | bytes 5588500
  319.6 8.8 %collective-permute-start.11 = (bf16[1,197,768]{2,1,0:T(8,128)(2,1)}, bf16[1,197,768]{2,1,0:T(8,128)(2,1)S(1)}, u32[]{:S(2)}, u32[]{:S(2)}) collective-permute-start(bf16[1,197,768]{2,1,0:T(8,128)(2,1)} %get-tuple-element.131), channel_id=1, source_target_pairs={{0,3},{1,0},{2,1},{3,2},{4,7},{5,4},{6,5},{7,6},{8,11},{9,8},{10,9... | collective-permute-start | bytes 907784 | tf_op jit(solution)/shard_map/ppermute | solution.py:341
  319.9 14.6 %collective-permute-start.10 = (bf16[1,197,768]{2,1,0:T(8,128)(2,1)}, bf16[1,197,768]{2,1,0:T(8,128)(2,1)}, u32[]{:S(2)}, u32[]{:S(2)}) collective-permute-start(bf16[1,197,768]{2,1,0:T(8,128)(2,1)} %get-tuple-element.132), channel_id=1, source_target_pairs={{0,2},{1,3},{2,0},{3,1},{4,6},{5,7},{6,4},{7,5},{8,10},{9,11},{10,... | collective-permute-start | bytes 907784 | tf_op jit(solution)/shard_map/ppermute | solution.py:341
  320.5 14.9 %collective-permute-start.9 = (bf16[1,197,768]{2,1,0:T(8,128)(2,1)}, bf16[1,197,768]{2,1,0:T(8,128)(2,1)}, u32[]{:S(2)}, u32[]{:S(2)}) collective-permute-start(bf16[1,197,768]{2,1,0:T(8,128)(2,1)} %get-tuple-element.130), channel_id=1, source_target_pairs={{0,1},{1,2},{2,3},{3,0},{4,5},{5,6},{6,7},{7,4},{8,9},{9,10},{10,1... | collective-permute-start | bytes 907784 | tf_op jit(solution)/shard_map/ppermute | solution.py:341
  326.4 9.0 %copy-start.6 = (bf16[1,197,768]{2,1,0:T(8,128)(2,1)S(1)}, bf16[1,197,768]{2,1,0:T(8,128)(2,1)}, u32[]{:S(2)}) copy-start(bf16[1,197,768]{2,1,0:T(8,128)(2,1)} %param.16) | copy-start | bytes 907780
  327.1 10.4 %copy-start.4 = (bf16[1,197,768]{2,1,0:T(8,128)(2,1)S(1)}, bf16[1,197,768]{2,1,0:T(8,128)(2,1)}, u32[]{:S(2)}) copy-start(bf16[1,197,768]{2,1,0:T(8,128)(2,1)} %param.31) | copy-start | bytes 907780
  327.1 10.4 %copy-start.8 = (f32[1,197,768]{2,1,0:T(8,128)S(1)}, f32[1,197,768]{2,1,0:T(8,128)}, u32[]{:S(2)}) copy-start(f32[1,197,768]{2,1,0:T(8,128)} %copy-done.7) | copy-start | bytes 1815556
  475.3 9.0 %collective-permute-start.12 = (f32[4,96]{0,1:T(8,128)}, f32[4,96]{0,1:T(8,128)}, u32[]{:S(2)}, u32[]{:S(2)}) collective-permute-start(f32[4,96]{0,1:T(8,128)} %slice_bitcast_fusion.14), channel_id=1, source_target_pairs={{0,0},{1,8},{2,16},{3,24},{4,1},{5,9},{6,17},{7,25},{8,2},{9,10},{... | collective-permute-start | bytes 4616 | tf_op jit(solution)/shard_map/ppermute | solution.py:609
  478.9 7.9 %copy-start.21 = (f32[4,96,768]{2,1,0:T(8,128)S(1)}, f32[4,96,768]{2,1,0:T(8,128)}, u32[]{:S(2)}) copy-start(f32[4,96,768]{2,1,0:T(8,128)} %get-tuple-element.29) | copy-start | bytes 3538948
  (30 other events, 96.7 us)
Sparse Core Ops, SparseCore 0:
  10.2 27.1 all-gather.3
  178.2 17.0 all-gather.5
  277.4 24.2 all-gather.7
